TPU v7x, 128 devices: a whole 4x4x4 slice. The times are simulated.
128 devices in a mesh: section: 8 (over y, core), ep: 16 (over z, x).
Axes of the slice: x: 4, y: 4, z: 4, core: 2. Of those that a mesh axis runs over, the one named last changes fastest.
Arguments:
- forward_input: bfloat16 [8, 2048, 2048], P('section', 'ep'), may hold values from -6 to 6
- backward_input: bfloat16 [8, 2048, 2048], P('section', 'ep'), may hold values from -6 to 6
- backward_grad: bfloat16 [8, 2048, 2048], P('section', 'ep'), may hold values from -6 to 6
- forward_routes: int32 [8, 2048, 2], P('section', 'ep'), may hold values from 0 to 31, all different within a row; in each aligned block of 128 rows (0 to 127, 128 to 255, ..., all dimensions but the last counted through in order) at most 24 rows name the same one
- backward_routes: int32 [8, 2048, 2], P('section', 'ep'), may hold values from 0 to 31, all different within a row; in each aligned block of 128 rows (0 to 127, 128 to 255, ..., all dimensions but the last counted through in order) at most 24 rows name the same one
- forward_times: int32 [8, 8], P('section'), may hold values from 0 to 15
- backward_times: int32 [8, 8], P('section'), may hold values from 0 to 15
- modulation: bfloat16 [8, 16, 3, 2048], P('section'), may hold values from -3 to 3
- router_weight: bfloat16 [8, 2048, 32], P('section'), may hold values from -0.125 to 0.125
- expert_up: bfloat16 [8, 32, 2048, 704], P('section', 'ep'), may hold values from -0.125 to 0.125
- expert_down: bfloat16 [8, 32, 704, 2048], P('section', 'ep'), may hold values from -0.21875 to 0.21875
Outputs:
- forward_output: bfloat16 [8, 2048, 2048], P('section', 'ep')
- input_grad: bfloat16 [8, 2048, 2048], P('section', 'ep')
- up_grad: bfloat16 [8, 32, 2048, 704], P('section', 'ep')
- down_grad: bfloat16 [8, 32, 704, 2048], P('section', 'ep')
- router_grad: float32 [8, 2048, 32], P('section')
- modulation_grad: float32 [8, 16, 3, 2048], P('section')
Inputs may be any that keep to these rules, and one draw needn't show every extreme that they name: `forward_routes`: in each device's 128 rows no expert is named by more than 24 rows and one expert by exactly 24; a token's two experts differ. `backward_routes`: as for forward_routes.
All inputs are finite; a program needn't handle non-finite values.
Results may differ from a plain program's by a relative error of at most 0.019.
Values may be sent and summed in bfloat16 or wider, within the bound.
A program may use at most 128 MiB of HBM per device.

v0:
```python
import jax
import jax.numpy as jnp
from jax import lax
from jax.sharding import PartitionSpec as P

PATCHES = 256


epsilon = 1e-06
highest = lax.Precision.HIGHEST


def passed_along(value, axis, steps):
    count = lax.axis_size(axis)
    pairs = [(source, (source + steps) % count) for source in range(count)]
    return lax.ppermute(value, axis, pairs)


def gelu_tanh(values):
    return jax.nn.gelu(values, approximate=True)


def gelu_slope(values):
    return jax.jvp(gelu_tanh, (values,), (jnp.ones_like(values),))[1]


def normalize(inputs):
    values = inputs.astype(jnp.float32)
    center = jnp.mean(values, axis=-1, keepdims=True)
    centered = values - center
    variance = jnp.mean(centered * centered, axis=-1, keepdims=True)
    inv_std = lax.rsqrt(variance + epsilon)
    return (centered * inv_std, inv_std)


def modulate(token_times, table):
    step_count = table.shape[0]
    onehot = (token_times[:, None] == jnp.arange(step_count, dtype=jnp.int32)[None, :]).astype(
        jnp.float32
    )
    flat = table.reshape(step_count, -1).astype(jnp.float32)
    return jnp.dot(onehot, flat, precision=highest).reshape(token_times.shape[0], 3, table.shape[2])


def slot_index(routes, expert_count, capacity):
    flat = routes.reshape(-1)
    onehot = (flat[:, None] == jnp.arange(expert_count, dtype=jnp.int32)[None, :]).astype(jnp.int32)
    ranks = jnp.sum((jnp.cumsum(onehot, axis=0) - 1) * onehot, axis=1)
    return (flat * capacity + ranks).reshape(routes.shape)


def top_gates(mixed_in, router, routes):
    logits = jnp.dot(mixed_in, router, preferred_element_type=jnp.float32)
    picked = jnp.take_along_axis(logits, routes, axis=1)
    first = jax.nn.sigmoid(picked[:, 0] - picked[:, 1])
    second = jax.nn.sigmoid(picked[:, 1] - picked[:, 0])
    return jnp.stack([first, second], axis=1)


def source_backward(
    grad_in,
    prob_grad,
    combined,
    slot_back,
    top_probs,
    routes,
    normed,
    inv_std,
    modulation_rows,
    mixed_in,
    router,
    token_times,
    step_count,
):
    logit_step = (prob_grad[:, 0] - prob_grad[:, 1]) * top_probs[:, 0] * top_probs[:, 1]
    expert_ids = jnp.arange(router.shape[1], dtype=jnp.int32)[None, :]
    selector = (routes[:, 0:1] == expert_ids).astype(jnp.float32) - (
        routes[:, 1:2] == expert_ids
    ).astype(jnp.float32)
    logit_grad = selector * logit_step[:, None]
    router_part = jnp.einsum(
        "td,te->de", mixed_in.astype(jnp.float32), logit_grad, precision=highest
    )
    mixed_grad = slot_back[:, 0].astype(jnp.float32) + slot_back[:, 1].astype(jnp.float32)
    mixed_grad = mixed_grad + jnp.einsum(
        "te,de->td", logit_grad, router.astype(jnp.float32), precision=highest
    )
    norm_grad = mixed_grad * (1.0 + modulation_rows[:, 1])
    grad_f = grad_in.astype(jnp.float32)
    input_part = grad_f + inv_std * (
        norm_grad
        - jnp.mean(norm_grad, axis=-1, keepdims=True)
        - normed * jnp.mean(norm_grad * normed, axis=-1, keepdims=True)
    )
    gate_term = grad_f * combined
    terms = jnp.stack([mixed_grad, mixed_grad * normed, gate_term], axis=1)
    onehot = (token_times[:, None] == jnp.arange(step_count, dtype=jnp.int32)[None, :]).astype(
        jnp.float32
    )
    table_part = jnp.dot(onehot.T, terms.reshape(terms.shape[0], -1), precision=highest).reshape(
        step_count, 3, -1
    )
    return (input_part.astype(jnp.bfloat16), router_part, table_part)


def prepare(inputs, times_img, routes, table, router, capacity):
    count = inputs.shape[0]
    token_ids = lax.axis_index("ep") * count + jnp.arange(count, dtype=jnp.int32)
    token_times = times_img[token_ids // PATCHES]
    modulation_rows = modulate(token_times, table)
    normed, inv_std = normalize(inputs)
    mixed_in = (normed * (1.0 + modulation_rows[:, 1]) + modulation_rows[:, 0]).astype(jnp.bfloat16)
    top_probs = top_gates(mixed_in, router, routes)
    slot_ids = slot_index(routes, router.shape[1], capacity)
    return (token_times, modulation_rows, normed, inv_std, mixed_in, top_probs, slot_ids)


def pack_slots(values, slot_ids, expert_count, capacity, owners):
    width = values.shape[-1]
    buffer = (
        jnp.zeros((expert_count * capacity, width), values.dtype)
        .at[slot_ids.reshape(-1)]
        .set(values.reshape(-1, width))
    )
    return buffer.reshape(owners, expert_count // owners, capacity, width)


def unpack_slots(buffer, slot_ids):
    width = buffer.shape[-1]
    return buffer.reshape(-1, width)[slot_ids]


def experts_local(slot_rows, up_w, down_w):
    pre_gelu = jnp.einsum("sjcd,jdf->sjcf", slot_rows, up_w, preferred_element_type=jnp.float32)
    hidden = gelu_tanh(pre_gelu).astype(jnp.bfloat16)
    expert_out = jnp.einsum(
        "sjcf,jfd->sjcd", hidden, down_w, preferred_element_type=jnp.float32
    ).astype(jnp.bfloat16)
    return (pre_gelu, hidden, expert_out)


def experts_backward(slot_mix, slot_prob, pre_gelu, up_w, down_w):
    out_grad = (slot_prob.astype(jnp.float32) * slot_mix.astype(jnp.float32)).astype(jnp.bfloat16)
    hidden_grad = jnp.einsum("sjcd,jfd->sjcf", out_grad, down_w, preferred_element_type=jnp.float32)
    pre_grad = (hidden_grad * gelu_slope(pre_gelu)).astype(jnp.bfloat16)
    slot_grad = jnp.einsum(
        "sjcf,jdf->sjcd", pre_grad, up_w, preferred_element_type=jnp.float32
    ).astype(jnp.bfloat16)
    return (out_grad, pre_grad, slot_grad)


def per_device(
    forward_input,
    backward_input,
    backward_grad,
    forward_routes,
    backward_routes,
    forward_times,
    backward_times,
    modulation,
    router_weight,
    expert_up,
    expert_down,
):
    table = modulation[0]
    router = router_weight[0]
    up_w = expert_up[0]
    down_w = expert_down[0]
    owners = lax.axis_size("ep")
    expert_count = router.shape[1]
    tok_count = forward_input.shape[1]
    capacity = max(2, 6 * tok_count // expert_count)
    width = forward_input.shape[2]
    step_count = table.shape[0]
    token_times, modulation_rows, normed, inv_std, mixed_in, top_probs, slot_ids = prepare(
        forward_input[0], forward_times[0], forward_routes[0], table, router, capacity
    )
    send_rows = pack_slots(
        jnp.broadcast_to(mixed_in[:, None, :], (tok_count, 2, width)),
        slot_ids,
        expert_count,
        capacity,
        owners,
    )
    unused_pre, unused_hidden, expert_out = experts_local(
        lax.all_to_all(send_rows, "ep", split_axis=0, concat_axis=0, tiled=True), up_w, down_w
    )
    returned = lax.all_to_all(expert_out, "ep", split_axis=0, concat_axis=0, tiled=True)
    gathered = unpack_slots(returned, slot_ids).astype(jnp.float32)
    combined = jnp.sum(top_probs[:, :, None] * gathered, axis=1)
    block_out = (forward_input[0].astype(jnp.float32) + modulation_rows[:, 2] * combined).astype(
        jnp.bfloat16
    )
    forward_output = passed_along(block_out, "section", 1)
    token_times, modulation_rows, normed, inv_std, mixed_in, top_probs, slot_ids = prepare(
        backward_input[0], backward_times[0], backward_routes[0], table, router, capacity
    )
    grad_in = backward_grad[0]
    mix_grad = (grad_in.astype(jnp.float32) * modulation_rows[:, 2]).astype(jnp.bfloat16)
    send_rows = pack_slots(
        jnp.broadcast_to(mixed_in[:, None, :], (tok_count, 2, width)),
        slot_ids,
        expert_count,
        capacity,
        owners,
    )
    send_second = pack_slots(
        jnp.broadcast_to(mix_grad[:, None, :], (tok_count, 2, width)),
        slot_ids,
        expert_count,
        capacity,
        owners,
    )
    send_third = pack_slots(
        top_probs.astype(jnp.bfloat16)[:, :, None], slot_ids, expert_count, capacity, owners
    )
    slot_rows = lax.all_to_all(send_rows, "ep", split_axis=0, concat_axis=0, tiled=True)
    second = lax.all_to_all(send_second, "ep", split_axis=0, concat_axis=0, tiled=True)
    third = lax.all_to_all(send_third, "ep", split_axis=0, concat_axis=0, tiled=True)
    pre_gelu, hidden, expert_out = experts_local(slot_rows, up_w, down_w)
    out_grad, pre_grad, slot_grad = experts_backward(second, third, pre_gelu, up_w, down_w)
    grad_back = lax.all_to_all(slot_grad, "ep", split_axis=0, concat_axis=0, tiled=True)
    out_back = lax.all_to_all(expert_out, "ep", split_axis=0, concat_axis=0, tiled=True)
    grad_back, second_back, slot_rows, hidden, out_grad, pre_grad = (
        grad_back,
        out_back,
        slot_rows,
        hidden,
        out_grad,
        pre_grad,
    )
    up_grad = jnp.einsum(
        "sjcd,sjcf->jdf", slot_rows, pre_grad, preferred_element_type=jnp.float32
    ).astype(jnp.bfloat16)
    down_grad = jnp.einsum(
        "sjcf,sjcd->jfd", hidden, out_grad, preferred_element_type=jnp.float32
    ).astype(jnp.bfloat16)
    slot_back = unpack_slots(grad_back, slot_ids)
    gathered_b = unpack_slots(second_back, slot_ids).astype(jnp.float32)
    prob_grad = jnp.sum(gathered_b * mix_grad.astype(jnp.float32)[:, None, :], axis=2)
    combined_b = jnp.sum(top_probs[:, :, None] * gathered_b, axis=1)
    input_part, router_part, table_part = source_backward(
        grad_in,
        prob_grad,
        combined_b,
        slot_back,
        top_probs,
        backward_routes[0],
        normed,
        inv_std,
        modulation_rows,
        mixed_in,
        router,
        token_times,
        step_count,
    )
    input_grad = passed_along(input_part, "section", -1)
    router_total, table_total = (
        lax.psum(router_part.astype(jnp.bfloat16), "ep").astype(jnp.float32),
        lax.psum(table_part.astype(jnp.bfloat16), "ep").astype(jnp.float32),
    )
    return (
        forward_output[None],
        input_grad[None],
        up_grad[None],
        down_grad[None],
        router_total[None],
        table_total[None],
    )


def solution(mesh):
    placed = (
        P("section", "ep", None),
        P("section", "ep", None),
        P("section", "ep", None),
        P("section", "ep", None),
        P("section", "ep", None),
        P("section", None),
        P("section", None),
        P("section", None, None, None),
        P("section", None, None),
        P("section", "ep", None, None),
        P("section", "ep", None, None),
    )
    return jax.shard_map(
        per_device,
        mesh=mesh,
        in_specs=placed,
        out_specs=(
            P("section", "ep", None),
            P("section", "ep", None),
            P("section", "ep", None, None),
            P("section", "ep", None, None),
            P("section", None, None),
            P("section", None, None, None),
        ),
        check_vma=False,
    )
```

profile of v0, /device:TPU:0, one launch (start us, length us, event | category | flops | bytes accessed | tf_op | source)
XLA Modules:
  0.0 469.3 jit_solution(2449524491951188553)
XLA Ops:
  15.6 5.1 %bitcast_select_fusion = s32[128]{0:T(128)S(1)} fusion(s32[]{:T(128)} %bitcast.42, s32[]{:T(128)} %bitcast.43, s32[]{:T(128)} %bitcast.44, s32[]{:T(128)} %bitcast.45, s32[]{:T(128)} %bitcast.46, s32[]{:T(128)} %bitcast.48, s32[]{:T(128)} %bitcast.47, s32[]{:T(128)} %bitcast.41, s32[]{:T(128)S(6)} %mul.263), kind=kLoop, calls=%fused_computation.190 | loop fusion | flops 4224 | bytes 548 | tf_op jit(solution)/shard_map/gather | solution.py:109
  29.2 8.0 %all-to-all-start.2 = ((bf16[16,2,24,1]{2,1,3,0:T(2,128)(2,1)}), bf16[16,2,24,1]{2,1,3,0:T(2,128)(2,1)S(1)}, u32[]{:S(2)}, u32[]{:S(2)}) async-start(bf16[16,2,24,1]{2,1,3,0:T(2,128)(2,1)} %bitcast.53), calls=%async_computation.2 | async-start | bytes 16384 | tf_op jit(solution)/shard_map/all_to_all | solution.py:219
  39.7 5.1 %bitcast_select_fusion.1 = s32[128]{0:T(128)S(1)} fusion(s32[]{:T(128)} %bitcast.3, s32[]{:T(128)} %bitcast.4, s32[]{:T(128)} %bitcast.5, s32[]{:T(128)} %bitcast.6, s32[]{:T(128)} %bitcast.7, s32[]{:T(128)} %bitcast.9, s32[]{:T(128)} %bitcast.8, s32[]{:T(128)} %bitcast.2, s32[]{:T(128)S(6)} %mul.263), kind=kLoop, calls=%fused_computation.191 | loop fusion | flops 4224 | bytes 548 | tf_op jit(solution)/shard_map/gather | solution.py:109
  53.8 7.5 %all-to-all-start = ((bf16[16,2,24,2048]{3,2,1,0:T(8,128)(2,1)}), bf16[16,2,24,2048]{3,2,1,0:T(8,128)(2,1)}, u32[]{:S(2)}, u32[]{:S(2)}) async-start(bf16[16,2,24,2048]{3,2,1,0:T(8,128)(2,1)} %bitcast.22), calls=%async_computation | async-start | bytes 6291456 | tf_op jit(solution)/shard_map/all_to_all | solution.py:186
  66.6 40.6 %all-to-all-done = bf16[16,2,24,2048]{3,2,1,0:T(8,128)(2,1)} async-done(((bf16[16,2,24,2048]{3,2,1,0:T(8,128)(2,1)}), bf16[16,2,24,2048]{3,2,1,0:T(8,128)(2,1)}, u32[]{:S(2)}, u32[]{:S(2)}) %all-to-all-start) | async-done | bytes 3145760 | tf_op jit(solution)/shard_map/all_to_all | solution.py:186
  107.2 4.5 all-to-all-start.3
  117.1 37.7 %all-to-all-done.3 = bf16[16,2,24,2048]{3,2,1,0:T(8,128)(2,1)} async-done(((bf16[16,2,24,2048]{3,2,1,0:T(8,128)(2,1)}), bf16[16,2,24,2048]{3,2,1,0:T(8,128)(2,1)}, u32[]{:S(2)}, u32[]{:S(2)}) %all-to-all-start.3) | async-done | bytes 3145760 | tf_op jit(solution)/shard_map/all_to_all | solution.py:218
  159.0 12.4 %fusion.33 = bf16[16,2,24,2048]{3,2,0,1:T(8,128)(2,1)} fusion(bf16[1,2,704,2048]{3,2,1,0:T(8,128)(2,1)} %param.23, bf16[1,2,2048,704]{2,3,1,0:T(8,128)(2,1)} %param.22, bf16[16,2,24,2048]{3,2,1,0:T(8,128)(2,1)} %all-to-all-done), kind=kOutput, calls=%fused_computation.39 | convolution fusion | flops 4435623936 | bytes 17825792 | tf_op jit(solution)/shard_map/sjcf,jfd->sjcd/dot_general | solution.py:136
  175.4 28.5 %all-to-all-done.4 = bf16[16,2,24,2048]{3,2,1,0:T(8,128)(2,1)S(1)} async-done(((bf16[16,2,24,2048]{3,2,1,0:T(8,128)(2,1)}), bf16[16,2,24,2048]{3,2,1,0:T(8,128)(2,1)S(1)}, u32[]{:S(2)}, u32[]{:S(2)}) %all-to-all-start.4) | async-done | bytes 3145760 | tf_op jit(solution)/shard_map/all_to_all | solution.py:217
  216.5 6.2 %fusion.4 = f32[2,16,24,704]{3,2,1,0:T(8,128)S(1)} fusion(bf16[1,2,2048,704]{2,3,1,0:T(8,128)(2,1)} %param.22, bf16[16,2,24,2048]{3,2,1,0:T(8,128)(2,1)} %copy-done.14), kind=kOutput, calls=%fused_computation.16 | convolution fusion | flops 2214592512 | bytes 11075584 | tf_op jit(solution)/shard_map/sjcd,jdf->sjcf/dot_general | solution.py:134
  222.7 6.7 %fusion.30 = bf16[16,2,24,2048]{3,2,0,1:T(8,128)(2,1)S(1)} fusion(bf16[1,2,704,2048]{3,2,1,0:T(8,128)(2,1)} %param.23, f32[2,16,24,704]{3,2,1,0:T(8,128)S(1)} %fusion.4), kind=kOutput, calls=%fused_computation.38 | convolution fusion | flops 2221031424 | bytes 11075584 | tf_op jit(solution)/shard_map/sjcf,jfd->sjcd/dot_general | solution.py:136
  231.4 20.1 %all-to-all-done.1 = bf16[16,2,24,2048]{3,2,1,0:T(8,128)(2,1)S(1)} async-done(((bf16[16,2,24,2048]{3,2,1,0:T(8,128)(2,1)}), bf16[16,2,24,2048]{3,2,1,0:T(8,128)(2,1)S(1)}, u32[]{:S(2)}, u32[]{:S(2)}) %all-to-all-start.1) | async-done | bytes 3145760 | tf_op jit(solution)/shard_map/all_to_all | solution.py:188
  251.5 4.7 all-to-all-start.6
  256.7 8.0 %fusion.49 = bf16[16,2,24,704]{3,2,0,1:T(8,128)(2,1)S(1)} fusion(f32[2,16,24,704]{3,2,1,0:T(8,128)} %copy-done.20, bf16[1,2,704,2048]{3,2,1,0:T(8,128)(2,1)} %param.23, bf16[16,2,24,2048]{3,2,1,0:T(8,128)(2,1)} %all-to-all-done.3, f32[16,2,24]{2,1,0:T(2,128)S(1)} %bitcast_convert_fusion.2), kind=kOutput, calls=%fused_computation.54 | convolution fusion | flops 2229043200 | bytes 12160000 | tf_op jit(solution)/shard_map/sjcd,jfd->sjcf/dot_general | solution.py:144
  264.7 5.9 %fusion.27 = bf16[16,2,24,2048]{3,2,0,1:T(8,128)(2,1)S(1)} fusion(bf16[16,2,24,704]{3,2,0,1:T(8,128)(2,1)S(1)} %fusion.49, bf16[1,2,2048,704]{2,3,1,0:T(8,128)(2,1)} %param.22), kind=kOutput, calls=%fused_computation.37 | convolution fusion | flops 2216165376 | bytes 9994240 | tf_op jit(solution)/shard_map/sjcf,jdf->sjcd/dot_general | solution.py:146
  272.5 27.6 %all-to-all-done.6 = bf16[16,2,24,2048]{3,2,1,0:T(8,128)(2,1)} async-done(((bf16[16,2,24,2048]{3,2,1,0:T(8,128)(2,1)}), bf16[16,2,24,2048]{3,2,1,0:T(8,128)(2,1)}, u32[]{:S(2)}, u32[]{:S(2)}) %all-to-all-start.6) | async-done | bytes 3145760 | tf_op jit(solution)/shard_map/all_to_all | solution.py:223
  300.1 4.5 all-to-all-start.5
  304.7 8.6 %fusion.1 = bf16[1,2,704,2048]{3,2,1,0:T(8,128)(2,1)} fusion(f32[2,16,24,704]{3,2,1,0:T(8,128)} %copy-done.20, bf16[16,2,24,2048]{3,2,1,0:T(8,128)(2,1)} %all-to-all-done.3, f32[16,2,24]{2,1,0:T(2,128)S(1)} %bitcast_convert_fusion.2), kind=kOutput, calls=%fused_computation.13 | convolution fusion | flops 2227060736 | bytes 11078656 | tf_op jit(solution)/shard_map/sjcf,sjcd->jfd/dot_general | solution.py:235
  323.6 4.7 gather_fusion.2
  329.7 6.2 %multiply_reduce_fusion = (f32[128,2048]{1,0:T(8,128)}, f32[128,2]{1,0:T(8,128)S(1)}) fusion(f32[128,2,2048]{2,1,0:T(2,128)S(1)} %reshape.665, f32[128,2]{1,0:T(8,128)S(1)} %copy.182, f32[128,2048]{1,0:T(8,128)} %get-tuple-element.13), kind=kLoop, calls=%fused_computation.69 | loop fusion | flops 1834752 | bytes 4196352 | tf_op jit(solution)/shard_map/reduce_sum | solution.py:241
  338.5 8.3 %all-to-all-done.5 = bf16[16,2,24,2048]{3,2,1,0:T(8,128)(2,1)} async-done(((bf16[16,2,24,2048]{3,2,1,0:T(8,128)(2,1)}), bf16[16,2,24,2048]{3,2,1,0:T(8,128)(2,1)}, u32[]{:S(2)}, u32[]{:S(2)}) %all-to-all-start.5) | async-done | bytes 3145760 | tf_op jit(solution)/shard_map/all_to_all | solution.py:222
  346.8 5.6 %gather_fusion.1 = bf16[256,2048]{1,0:T(8,128)(2,1)} fusion(bf16[768,2048]{1,0:T(8,128)(2,1)} %bitcast.64, s32[1024]{0:T(1024)S(1)} %pad_clamp_fusion), kind=kCustom, calls=%fused_computation.3 | custom fusion | bytes 2098176 | tf_op jit(solution)/shard_map/gather | solution.py:130
  372.6 7.9 %fusion = bf16[1,2,2048,704]{2,3,1,0:T(8,128)(2,1)} fusion(bf16[16,2,24,2048]{3,2,1,0:T(8,128)(2,1)} %copy-done.14, bf16[16,2,24,704]{3,2,0,1:T(8,128)(2,1)} %copy-done.19), kind=kOutput, calls=%fused_computation.12 | convolution fusion | flops 2217476096 | bytes 9994240 | tf_op jit(solution)/shard_map/sjcd,sjcf->jdf/dot_general | solution.py:232
  380.5 74.4 %all-reduce.3.cloned.1.call-done = (bf16[1,2048,32]{1,2,0:T(8,128)(2,1)}, bf16[1,16,3,2048]{3,1,2,0:T(8,128)(2,1)}) async-done(((bf16[1,2048,32]{1,2,0:T(8,128)(2,1)}, bf16[1,16,3,2048]{3,1,2,0:T(8,128)(2,1)}), (bf16[1,2048,32]{1,2,0:T(8,128)(2,1)}, bf16[1,16,3,2048]{3,1,2,0:T(8,128)(2,1)})) %all-reduce.3.cloned.1.call-update) | async-done | bytes 327696 | tf_op jit(solution)/shard_map/psum | solution.py:259
  (163 shorter events, 105.2 us)
Async XLA Ops:
  7.2 16.2 %copy-start = (bf16[1,2048,32]{1,2,0:T(8,128)(2,1)S(1)}, bf16[1,2048,32]{1,2,0:T(8,128)(2,1)}, u32[]{:S(2)}) copy-start(bf16[1,2048,32]{1,2,0:T(8,128)(2,1)} %param.21) | copy-start | bytes 393220
  7.2 14.2 %copy-start.6 = (bf16[1,128,2048]{2,1,0:T(8,128)(2,1)S(1)}, bf16[1,128,2048]{2,1,0:T(8,128)(2,1)}, u32[]{:S(2)}) copy-start(bf16[1,128,2048]{2,1,0:T(8,128)(2,1)} %param.14) | copy-start | bytes 1572868
  7.2 14.2 %copy-start.10 = (bf16[1,128,2048]{2,1,0:T(8,128)(2,1)S(1)}, bf16[1,128,2048]{2,1,0:T(8,128)(2,1)}, u32[]{:S(2)}) copy-start(bf16[1,128,2048]{2,1,0:T(8,128)(2,1)} %param.15) | copy-start | bytes 1572868
  14.3 8.9 %copy-start.18 = (s32[32,3]{0,1:T(4,128)}, s32[32,3]{0,1:T(4,128)S(1)}, u32[]{:S(2)}) copy-start(s32[32,3]{0,1:T(4,128)S(1)} %reduce-window.19) | copy-start | bytes 1156
  23.6 13.5 %copy-start.17 = (s32[1,128,2]{1,2,0:T(2,128)S(1)}, s32[1,128,2]{1,2,0:T(2,128)}, u32[]{:S(2)}) copy-start(s32[1,128,2]{1,2,0:T(2,128)} %param.16) | copy-start | bytes 3076
  23.6 13.9 %copy-start.4 = (bf16[1,128,2048]{2,1,0:T(8,128)(2,1)S(1)}, bf16[1,128,2048]{2,1,0:T(8,128)(2,1)}, u32[]{:S(2)}) copy-start(bf16[1,128,2048]{2,1,0:T(8,128)(2,1)} %param.13) | copy-start | bytes 1572868
  23.7 14.4 %copy-start.15 = (s32[1,8]{1,0:T(1,128)S(1)}, s32[1,8]{1,0:T(1,128)}, u32[]{:S(2)}) copy-start(s32[1,8]{1,0:T(1,128)} %param.18) | copy-start | bytes 100
  29.2 24.6 %all-to-all-start.2 = ((bf16[16,2,24,1]{2,1,3,0:T(2,128)(2,1)}), bf16[16,2,24,1]{2,1,3,0:T(2,128)(2,1)S(1)}, u32[]{:S(2)}, u32[]{:S(2)}) async-start(bf16[16,2,24,1]{2,1,3,0:T(2,128)(2,1)} %bitcast.53), calls=%async_computation.2 | async-start | bytes 16384 | tf_op jit(solution)/shard_map/all_to_all | solution.py:219
  53.8 53.5 %all-to-all-start = ((bf16[16,2,24,2048]{3,2,1,0:T(8,128)(2,1)}), bf16[16,2,24,2048]{3,2,1,0:T(8,128)(2,1)}, u32[]{:S(2)}, u32[]{:S(2)}) async-start(bf16[16,2,24,2048]{3,2,1,0:T(8,128)(2,1)} %bitcast.22), calls=%async_computation | async-start | bytes 6291456 | tf_op jit(solution)/shard_map/all_to_all | solution.py:186
  107.2 47.6 %all-to-all-start.3 = ((bf16[16,2,24,2048]{3,2,1,0:T(8,128)(2,1)}), bf16[16,2,24,2048]{3,2,1,0:T(8,128)(2,1)}, u32[]{:S(2)}, u32[]{:S(2)}) async-start(bf16[16,2,24,2048]{3,2,1,0:T(8,128)(2,1)} %bitcast.57), calls=%async_computation.3 | async-start | bytes 6291456 | tf_op jit(solution)/shard_map/all_to_all | solution.py:218
  154.8 49.2 %all-to-all-start.4 = ((bf16[16,2,24,2048]{3,2,1,0:T(8,128)(2,1)}), bf16[16,2,24,2048]{3,2,1,0:T(8,128)(2,1)S(1)}, u32[]{:S(2)}, u32[]{:S(2)}) async-start(bf16[16,2,24,2048]{3,2,1,0:T(8,128)(2,1)} %bitcast.60), calls=%async_computation.4 | async-start | bytes 6291456 | tf_op jit(solution)/shard_map/all_to_all | solution.py:217
  205.7 45.8 %all-to-all-start.1 = ((bf16[16,2,24,2048]{3,2,1,0:T(8,128)(2,1)}), bf16[16,2,24,2048]{3,2,1,0:T(8,128)(2,1)S(1)}, u32[]{:S(2)}, u32[]{:S(2)}) async-start(bf16[16,2,24,2048]{3,2,1,0:T(8,128)(2,1)} %copy.162), calls=%async_computation.1 | async-start | bytes 6291456 | tf_op jit(solution)/shard_map/all_to_all | solution.py:188
  222.7 6.7 %copy-start.20 = (f32[2,16,24,704]{3,2,1,0:T(8,128)}, f32[2,16,24,704]{3,2,1,0:T(8,128)S(1)}, u32[]{:S(2)}) copy-start(f32[2,16,24,704]{3,2,1,0:T(8,128)S(1)} %fusion.4) | copy-start | bytes 6488068
  251.5 48.7 %all-to-all-start.6 = ((bf16[16,2,24,2048]{3,2,1,0:T(8,128)(2,1)}), bf16[16,2,24,2048]{3,2,1,0:T(8,128)(2,1)}, u32[]{:S(2)}, u32[]{:S(2)}) async-start(bf16[16,2,24,2048]{3,2,1,0:T(8,128)(2,1)} %copy.177), calls=%async_computation.6 | async-start | bytes 6291456 | tf_op jit(solution)/shard_map/all_to_all | solution.py:223
  264.7 5.9 %copy-start.19 = (bf16[16,2,24,704]{3,2,0,1:T(8,128)(2,1)}, bf16[16,2,24,704]{3,2,0,1:T(8,128)(2,1)S(1)}, u32[]{:S(2)}) copy-start(bf16[16,2,24,704]{3,2,0,1:T(8,128)(2,1)S(1)} %fusion.49) | copy-start | bytes 3244036
  300.1 46.7 %all-to-all-start.5 = ((bf16[16,2,24,2048]{3,2,1,0:T(8,128)(2,1)}), bf16[16,2,24,2048]{3,2,1,0:T(8,128)(2,1)}, u32[]{:S(2)}, u32[]{:S(2)}) async-start(bf16[16,2,24,2048]{3,2,1,0:T(8,128)(2,1)} %copy.174), calls=%async_computation.5 | async-start | bytes 6291456 | tf_op jit(solution)/shard_map/all_to_all | solution.py:222
  304.6 150.3 %all-reduce.3.cloned.1.call-start = ((), (), s32[]{:S(2)}) async-start(), calls=%async_computation.7 | async-start | bytes 655360 | tf_op jit(solution)/shard_map/psum | solution.py:259
  315.7 5.7 %copy-start.5 = (bf16[1,128,2048]{2,1,0:T(8,128)(2,1)S(1)}, bf16[1,128,2048]{2,1,0:T(8,128)(2,1)}, u32[]{:S(2)}) copy-start(bf16[1,128,2048]{2,1,0:T(8,128)(2,1)} %param.13) | copy-start | bytes 1572868
  323.6 134.7 %collective-permute-start = (bf16[128,2048]{1,0:T(8,128)(2,1)}, bf16[128,2048]{1,0:T(8,128)(2,1)}, u32[]{:S(2)}, u32[]{:S(2)}) collective-permute-start(bf16[128,2048]{1,0:T(8,128)(2,1)} %fusion.98), channel_id=1, source_target_pairs={{0,16},{16,32},{32,48},{48,64},{64,80},{80,96},{96,112},{112,0},{1... | collective-permute-start | bytes 1572872 | tf_op jit(solution)/shard_map/ppermute | solution.py:16
  329.6 6.5 %copy-start.11 = (bf16[1,128,2048]{2,1,0:T(8,128)(2,1)S(1)}, bf16[1,128,2048]{2,1,0:T(8,128)(2,1)}, u32[]{:S(2)}) copy-start(bf16[1,128,2048]{2,1,0:T(8,128)(2,1)} %param.15) | copy-start | bytes 1572868
  352.4 6.4 %copy-start.2 = (f32[128,3,2048]{2,0,1:T(8,128)S(1)}, f32[128,3,2048]{2,0,1:T(8,128)}, u32[]{:S(2)}) copy-start(f32[128,3,2048]{2,0,1:T(8,128)} %copy-done.1) | copy-start | bytes 9437188
  355.3 5.0 %copy-start.12 = (bf16[1,128,2048]{2,1,0:T(8,128)(2,1)S(1)}, bf16[1,128,2048]{2,1,0:T(8,128)(2,1)}, u32[]{:S(2)}) copy-start(bf16[1,128,2048]{2,1,0:T(8,128)(2,1)} %param.15) | copy-start | bytes 1572868
  367.1 4.1 copy-start.8
  371.2 87.0 %collective-permute-start.1 = (bf16[128,2048]{1,0:T(8,128)(2,1)}, bf16[128,2048]{1,0:T(8,128)(2,1)}, u32[]{:S(2)}, u32[]{:S(2)}) collective-permute-start(bf16[128,2048]{1,0:T(8,128)(2,1)} %get-tuple-element.17), channel_id=1, source_target_pairs={{0,112},{16,0},{32,16},{48,32},{64,48},{80,64},{96,80},{112,96},{1... | collective-permute-start | bytes 1572872 | tf_op jit(solution)/shard_map/ppermute | solution.py:16
  (8 other events, 15.8 us)
Sparse Core Ops, SparseCore 0:
  372.7 82.2 all-reduce.2
where the time goes:
time: 479 us; the launch traced here: 469 us
  waiting for transfers between devices  237 us (49%)
  local copies, waits for them, and re-layouts  74 us (15%)
  matrix products  65.6 us (14%)
  other arithmetic  40.1 us (8%)
  starting transfers between devices  37.1 us (8%)
  between operations  15.1 us (3%)
    psum x1, waiting for transfers between devices, per_device(): lax.psum(router_part.astype(jnp.bfloat16), 'ep').astype(jnp.float32)  74.4 us
    all_to_all x2, waiting for transfers between devices, per_device(): lax.all_to_all(send_rows, 'ep', split_axis=0, concat_axis=0, tiled=True)  69.1 us
    all_to_all x2, waiting for transfers between devices, per_device(): lax.all_to_all(expert_out, 'ep', split_axis=0, concat_axis=0, tiled=True)  47.7 us
    all_to_all x1, waiting for transfers between devices, per_device(): lax.all_to_all(send_second, 'ep', split_axis=0, concat_axis=0, tiled=True)  37.7 us
    dot_general x2, matrix products, experts_local(): jnp.einsum('sjcf,jfd->sjcd', hidden, down_w, preferred_element_type=jnp.f...  19.2 us
    gather x4, local copies, waits for them, and re-layouts, unpack_slots(): return buffer.reshape(-1, width)[slot_ids]  15.5 us
    scatter x4, local copies, waits for them, and re-layouts, pack_slots(): buffer = jnp.zeros((expert_count * capacity, width), values.dtype).at[slo...  15 us
    all_to_all x2, starting transfers between devices, per_device(): lax.all_to_all(send_rows, 'ep', split_axis=0, concat_axis=0, tiled=True)  11.7 us
  transfers between devices with their start and end apart: 10, of which 7 were waited for; matrix products, arithmetic and copies ran while one was open for 32% of the time, Pallas kernels for 0%

commit v1 on v0

v1 whole, which is shorter than its diff:
```python
import jax
import jax.numpy as jnp
from jax import lax
from jax.experimental import pallas as pl
from jax.experimental.pallas import tpu as pltpu
from jax.sharding import PartitionSpec as P

D = 2048
HALF = 1024
FF = 704
TOK = 128
CAP = 24
SLOT = 2 * CAP
EXPERTS = 32
IMAGES = 8
ROWS = IMAGES * SLOT
STAT = 56
TILE = 512
epsilon = 1e-06
MESH = pl.DeviceIdType.MESH
f32 = jnp.float32
bf16 = jnp.bfloat16
FF_TILES = ((0, 256), (256, 512), (512, 704))
PROB, PROB2, OTHER, MU, ISTD, PGRAD = (slice(k, k + 1) for k in range(6))
GELU_A = 0.7978845608028654
GELU_B = 0.044715


def dot(a, b):
    return jnp.dot(a, b, preferred_element_type=f32)


def dot_nt(a, b):
    return lax.dot_general(a, b, (((1,), (1,)), ((), ())), preferred_element_type=f32)


def dot_tn(a, b):
    return lax.dot_general(a, b, (((0,), (0,)), ((), ())), preferred_element_type=f32)


def gelu(values):
    inner = jnp.tanh(GELU_A * (values + GELU_B * values * values * values))
    return 0.5 * values * (1.0 + inner)


def gelu_slope(values):
    square = values * values
    inner = jnp.tanh(GELU_A * (values + GELU_B * values * square))
    outer = 0.5 * values * (1.0 - inner * inner) * (GELU_A * (1.0 + 3.0 * GELU_B * square))
    return 0.5 * (1.0 + inner) + outer


def loop(count, body):
    def step(index, carry):
        body(index)
        return carry

    lax.fori_loop(0, count, step, 0)


class Sems:
    def __init__(self, send, recv, local):
        self.send, self.recv, self.local = send, recv, local
        self.remote_used = self.local_used = 0

    def remote(self, src, dst, device):
        k = self.remote_used
        self.remote_used += 1
        return pltpu.make_async_remote_copy(
            src_ref=src,
            dst_ref=dst,
            send_sem=self.send.at[k],
            recv_sem=self.recv.at[k],
            device_id=device,
            device_id_type=MESH,
        )

    def copy(self, src, dst):
        k = self.local_used
        self.local_used += 1
        return pltpu.make_async_copy(src, dst, self.local.at[k])


N_REMOTE = 110
N_LOCAL = 40


def layer_kernel(
    routes_f,
    routes_b,
    times_f,
    times_b,
    table_ref,
    router_ref,
    xf_hbm,
    xb_hbm,
    dy_hbm,
    up_hbm,
    down_hbm,
    out_f,
    out_b,
    xm_out,
    og_out,
    hid_out,
    pg_out,
    fin_out,
    send_sem,
    recv_sem,
    local_sem,
    meta,
    onehot,
    ag_xb,
    ag_dy,
    ag_xf,
    sb_0,
    sb_1,
    sl_xb,
    sl_dy,
    sl_xf,
    rr_b,
    rr_f,
    hop_b,
    hop_f,
    last_b,
    last_f,
    own,
    up,
    down,
    xm,
    og,
    pre,
    hid,
    pgr,
    tile_out,
    modr,
    cols,
    wrow,
    stat,
    st_z,
    st_2,
    st_x,
    fin,
    res,
):
    section = lax.axis_index("section")
    me = lax.axis_index("ep")
    z, x = me // 4, me % 4
    sems = Sems(send_sem, recv_sem, local_sem)

    def peer(axis, off):
        if axis == 0:
            return (section, lax.rem(z + off + 4, 4) * 4 + x)
        return (section, z * 4 + lax.rem(x + off + 4, 4))

    spot = (z, x)

    def at(axis, off):
        return lax.rem(spot[axis] + off + 4, 4)

    own_copies = []
    for source, ag in ((xb_hbm, ag_xb), (dy_hbm, ag_dy), (xf_hbm, ag_xf)):
        for h in (0, 1):
            cp = sems.copy(source.at[0, :, pl.ds(h * HALF, HALF)], ag.at[h, spot[h]])
            cp.start()
            own_copies.append(cp)
    up_copy = sems.copy(up_hbm.at[0], up)
    down_copy = sems.copy(down_hbm.at[0], down)
    up_copy.start()
    down_copy.start()

    expert_rows = lax.broadcasted_iota(jnp.int32, (EXPERTS, TOK), 0).astype(f32)
    earlier = (
        lax.broadcasted_iota(jnp.int32, (TOK, TOK), 0)
        < lax.broadcasted_iota(jnp.int32, (TOK, TOK), 1)
    ).astype(bf16)
    for way in (0, 1):
        routes = routes_b if way else routes_f
        e0 = routes[0:1, :].astype(f32)
        e1 = routes[1:2, :].astype(f32)
        o0 = (expert_rows == e0).astype(f32)
        o1 = (expert_rows == e1).astype(f32)
        rank = dot((o0 + o1).astype(bf16), earlier)
        s0 = e0 * CAP + jnp.sum(o0 * rank, axis=0, keepdims=True)
        s1 = e1 * CAP + jnp.sum(o1 * rank, axis=0, keepdims=True)
        for k, row in enumerate((s0, s1, e0, e1)):
            meta[x, z, 4 * way + k : 4 * way + k + 1, :] = row

    barrier = pltpu.get_barrier_semaphore()
    for axis in (0, 1):
        for off in (1, 2, 3):
            pl.semaphore_signal(barrier, inc=1, device_id=peer(axis, off), device_id_type=MESH)
    pl.semaphore_wait(barrier, 6)

    meta_z = [sems.remote(meta.at[x, z], meta.at[x, z], peer(0, off)) for off in (1, 2, 3)]
    for cp in meta_z:
        cp.start()

    for cp in own_copies:
        cp.wait()

    def gather_start(ag):
        copies = []
        for off in (1, 3):
            for h in (0, 1):
                block = ag.at[h, spot[h]]
                cp = sems.remote(block, block, peer(h, off))
                cp.start()
                copies.append(cp)
        return copies

    def gather_forward(ag, first):
        copies = []
        for k, off in enumerate((1, 3)):
            for h in (0, 1):
                first[2 * k + h].wait_recv()
                block = ag.at[h, at(h, -off), pl.ds(64 * k, 64)]
                cp = sems.remote(block, block, peer(h, off))
                cp.start()
                copies.append(cp)
        return copies

    g_xb = gather_start(ag_xb)
    g_dy = gather_start(ag_dy)

    for cp in meta_z:
        cp.wait()
    meta_x = [sems.remote(meta.at[x], meta.at[x], peer(1, off)) for off in (1, 2, 3)]
    for cp in meta_x:
        cp.start()

    time_rows = lax.broadcasted_iota(jnp.int32, (2 * IMAGES, 16), 0)
    time_of = jnp.zeros((2 * IMAGES, 16), jnp.int32)
    for i in range(IMAGES):
        time_of = jnp.where(time_rows == i, times_f[0, i], time_of)
        time_of = jnp.where(time_rows == IMAGES + i, times_b[0, i], time_of)
    chosen = (time_of == lax.broadcasted_iota(jnp.int32, (2 * IMAGES, 16), 1)).astype(f32)
    for c in range(3):
        modr[c] = dot(chosen.astype(bf16), table_ref[0, c])

    def modulation_of(way, i, c, span=slice(0, D)):
        return modr[c, pl.ds(i + IMAGES * way, 1), span]

    slot_rows = lax.broadcasted_iota(jnp.int32, (4 * SLOT, TOK), 0)

    def build_onehot(way, h):
        if h == 0:
            ids = slot_rows + z * 192
        else:
            block = (
                (slot_rows >= 48).astype(jnp.int32)
                + (slot_rows >= 96).astype(jnp.int32)
                + (slot_rows >= 144).astype(jnp.int32)
            )
            ids = slot_rows + block * 144 + x * SLOT
        ids = ids.astype(f32)

        def one(s):
            block = meta[x, s] if h == 0 else meta[s, z]
            s0 = block[4 * way : 4 * way + 1, :]
            s1 = block[4 * way + 1 : 4 * way + 2, :]
            onehot[way, h, s] = ((ids == s0).astype(f32) + (ids == s1).astype(f32)).astype(bf16)

        loop(4, one)

    build_onehot(1, 0)
    for cp in meta_x:
        cp.wait()
    build_onehot(1, 1)
    build_onehot(0, 0)
    build_onehot(0, 1)

    def pack(way, ag, sb, h):
        def one(s):
            for n in (0, 1):
                part = dot(onehot[way, h, s], ag[h, s, :, n * TILE : (n + 1) * TILE])
                sb[h, :, s, :, n * TILE : (n + 1) * TILE] = part.astype(bf16).reshape(4, SLOT, TILE)

        loop(4, one)

    def exchange(sb, rb):
        copies = []
        for off in (2, 1, 3):
            for h in (0, 1):
                axis = 1 - h
                cp = sems.remote(
                    sb.at[h, at(axis, off)], rb.at[h, spot[axis]], peer(axis, off)
                )
                cp.start()
                copies.append(cp)
        local = []
        for h in (0, 1):
            axis = 1 - h
            cp = sems.copy(sb.at[h, spot[axis]], rb.at[h, spot[axis]])
            cp.start()
            local.append(cp)
        return copies, local

    def arrived(copies):
        for cp in copies[0]:
            cp.wait_recv()
        for cp in copies[1]:
            cp.wait()

    def dispatch_pack(way, ag, first, second, sb, rb):
        for cp in second:
            cp.wait_recv()
        for h in (0, 1):
            pack(way, ag, sb, h)
        return exchange(sb, rb)

    f_xb = gather_forward(ag_xb, g_xb)
    g_xf = gather_start(ag_xf)
    a_xb = dispatch_pack(1, ag_xb, g_xb, f_xb, sb_0, sl_xb)
    f_dy = gather_forward(ag_dy, g_dy)
    a_dy = dispatch_pack(1, ag_dy, g_dy, f_dy, sb_1, sl_dy)
    f_xf = gather_forward(ag_xf, g_xf)
    for cp in a_xb[0]:
        cp.wait_send()
    for cp in a_xb[1]:
        cp.wait()
    a_xf = dispatch_pack(0, ag_xf, g_xf, f_xf, sb_0, sl_xf)
    for cp in g_xb + f_xb + g_dy + f_dy + g_xf + f_xf:
        cp.wait_send()

    def slots_of(sl, h, zi, xi):
        block = sl[h, xi, zi] if h == 0 else sl[h, zi, xi]
        return block.astype(f32)

    def by_expert(sl, h, i, j):
        zi, xi = i // 2, 2 * (i % 2)
        first = slots_of(sl, h, zi, xi)[j * CAP : (j + 1) * CAP]
        second = slots_of(sl, h, zi, xi + 1)[j * CAP : (j + 1) * CAP]
        return jnp.concatenate([first, second], axis=0)

    cap_rows = lax.broadcasted_iota(jnp.int32, (CAP, TOK), 0)

    def normalize(sl, way):
        def one(i):
            zi, xi = i // 2, 2 * (i % 2)
            shift, scale = modulation_of(way, i, 0), modulation_of(way, i, 1)
            for j in (0, 1):
                left, right = by_expert(sl, 0, i, j), by_expert(sl, 1, i, j)
                total = jnp.sum(left, axis=1, keepdims=True) + jnp.sum(right, axis=1, keepdims=True)
                center = total * (1.0 / D)
                left, right = left - center, right - center
                total = jnp.sum(left * left, axis=1, keepdims=True) + jnp.sum(
                    right * right, axis=1, keepdims=True
                )
                inv = lax.rsqrt(total * (1.0 / D) + epsilon)
                for h, part in ((0, left), (1, right)):
                    span = slice(h * HALF, (h + 1) * HALF)
                    mixed = part * inv * (1.0 + scale[:, span]) + shift[:, span]
                    xm[j, i, :, span] = mixed.astype(bf16)
                cols[j, i, :, MU] = center
                cols[j, i, :, ISTD] = inv
                ids = (cap_rows + (me * SLOT + j * CAP)).astype(f32)
                found = []
                for par in (0, 1):
                    block = meta[xi + par, zi]
                    s0, s1, e0, e1 = [
                        block[4 * way + k : 4 * way + k + 1, :] for k in range(4)
                    ]
                    hit = jnp.where(ids == s0, e1, 0.0) + jnp.where(ids == s1, e0, 0.0)
                    found.append(jnp.sum(hit, axis=1, keepdims=True))
                cols[j, i, :, OTHER] = jnp.concatenate(found, axis=0)

        loop(IMAGES, one)

    lane = lax.broadcasted_iota(jnp.int32, (ROWS, EXPERTS), 1)

    def picks(j):
        own = (lane == 2 * me + j).astype(f32)
        return own - (lane.astype(f32) == cols[j, :, :, OTHER].reshape(ROWS, 1)).astype(f32)

    def experts_up(keep):
        def one(j):
            rows = xm[j].reshape(ROWS, D)
            logits = dot_nt(rows, router_ref[0])
            gap = jnp.sum(logits * picks(j), axis=1, keepdims=True)
            chance = 1.0 / (1.0 + jnp.exp(-gap))
            cols[j, :, :, PROB] = chance.reshape(IMAGES, SLOT, 1)
            if keep:
                cols[j, :, :, PROB2] = (chance * (1.0 / (1.0 + jnp.exp(gap)))).reshape(IMAGES, SLOT, 1)
            for f0, f1 in FF_TILES:
                part = dot_nt(rows, up[j, f0:f1, :])
                if keep:
                    pre[j, :, f0:f1] = part
                hid[j, :, f0:f1] = gelu(part).astype(bf16)

        loop(2, one)

    def put_rows(sb, h, n):
        def one(i):
            zi, xi = i // 2, 2 * (i % 2)
            a, b = tile_out[0, i], tile_out[1, i]
            for par in (0, 1):
                block = jnp.concatenate(
                    [a[par * CAP : (par + 1) * CAP], b[par * CAP : (par + 1) * CAP]], axis=0
                ).astype(bf16)
                span = slice(n * TILE, (n + 1) * TILE)
                if h == 0:
                    sb[h, xi + par, zi, :, span] = block
                else:
                    sb[h, zi, xi + par, :, span] = block

        loop(IMAGES, one)

    for cp in a_xb[0]:
        cp.wait_recv()
    normalize(sl_xb, 1)
    up_copy.wait()
    experts_up(True)
    down_copy.wait()
    arrived(a_dy)

    stat[...] = jnp.zeros_like(stat)
    cols[:, :, :, PGRAD] = jnp.zeros((2, IMAGES, SLOT, 1), f32)

    def order_dy(i):
        for j in (0, 1):
            for h in (0, 1):
                og[j, i, :, h * HALF : (h + 1) * HALF] = by_expert(sl_dy, h, i, j).astype(bf16)

    loop(IMAGES, order_dy)

    for n in range(D // TILE):
        span = slice(n * TILE, (n + 1) * TILE)

        def out_tile(j):
            part = dot(hid[j], down[j, :, span]).astype(bf16).astype(f32)
            tile_out[j] = part.reshape(IMAGES, SLOT, TILE)

        loop(2, out_tile)

        def out_image(i):
            gate = modulation_of(1, i, 2, span)
            total = jnp.zeros((1, TILE), f32)
            for j in (0, 1):
                out = tile_out[j, i]
                dyv = og[j, i, :, span].astype(f32)
                chance = cols[j, i, :, PROB]
                mix = (dyv * gate).astype(bf16).astype(f32)
                cols[j, i, :, PGRAD] += jnp.sum(out * mix, axis=1, keepdims=True)
                total += jnp.sum(out * dyv * chance, axis=0, keepdims=True)
                og[j, i, :, span] = (chance.astype(bf16).astype(f32) * mix).astype(bf16)
            stat[2, pl.ds(i, 1), span] = total

        loop(IMAGES, out_image)

    def hidden_grad(j):
        rows = og[j].reshape(ROWS, D)
        for f0, f1 in FF_TILES:
            part = dot_nt(rows, down[j, f0:f1, :])
            pgr[j, :, f0:f1] = (part * gelu_slope(pre[j, :, f0:f1])).astype(bf16)
        weight = picks(j) * (cols[j, :, :, PGRAD] * cols[j, :, :, PROB2]).reshape(ROWS, 1)
        high = weight.astype(bf16)
        wrow[j, 0] = high
        wrow[j, 1] = (weight - high.astype(f32)).astype(bf16)

    loop(2, hidden_grad)
    for cp in a_dy[0]:
        cp.wait_send()

    for n in range(D // TILE):
        h = n // 2
        span = slice(n * TILE, (n + 1) * TILE)

        def grad_tile(j):
            part = dot(pgr[j], up[j, :, span]).astype(bf16).astype(f32)
            rows = router_ref[0, :, span]
            part += dot(wrow[j, 0], rows) + dot(wrow[j, 1], rows)
            tile_out[j] = part.reshape(IMAGES, SLOT, TILE)
            block = xm[j].reshape(ROWS, D)[:, span]
            rg = dot_tn(wrow[j, 0], block) + dot_tn(wrow[j, 1], block)
            for k in range(EXPERTS // 8):
                stat[3 + k, :, span] += rg[8 * k : 8 * k + 8]

        loop(2, grad_tile)
        inner = slice((n % 2) * TILE, (n % 2 + 1) * TILE)

        def grad_image(i):
            zi, xi = i // 2, 2 * (i % 2)
            shift = jnp.zeros((1, TILE), f32)
            scale = jnp.zeros((1, TILE), f32)
            for par in (0, 1):
                block = sl_xb[h, xi + par, zi, :, inner] if h == 0 else sl_xb[h, zi, xi + par, :, inner]
                block = block.astype(f32)
                for j in (0, 1):
                    cut = slice(par * CAP, (par + 1) * CAP)
                    grad = tile_out[j, i][cut]
                    normed = (block[j * CAP : (j + 1) * CAP] - cols[j, i, cut, MU]) * cols[j, i, cut, ISTD]
                    shift += jnp.sum(grad, axis=0, keepdims=True)
                    scale += jnp.sum(grad * normed, axis=0, keepdims=True)
            stat[0, pl.ds(i, 1), span] = shift
            stat[1, pl.ds(i, 1), span] = scale

        loop(IMAGES, grad_image)
        put_rows(sb_1, h, n % 2)

    r_b = exchange(sb_1, rr_b)
    kept = []
    for source, dest in ((xm, xm_out), (og, og_out), (hid, hid_out), (pgr, pg_out)):
        cp = sems.copy(source, dest)
        cp.start()
        kept.append(cp)
    sum_z = [
        sems.remote(
            stat.at[:, :, pl.ds(pl.multiple_of(at(0, off) * TILE, TILE), TILE)],
            st_z.at[z],
            peer(0, off),
        )
        for off in (1, 2, 3)
    ]
    for cp in sum_z:
        cp.start()

    arrived(a_xf)
    for cp in kept:
        cp.wait()
    normalize(sl_xf, 0)
    experts_up(False)
    for cp in a_xf[0]:
        cp.wait_send()
    for n in range(D // TILE):
        span = slice(n * TILE, (n + 1) * TILE)

        def give_tile(j):
            part = dot(hid[j], down[j, :, span]) * cols[j, :, :, PROB].reshape(ROWS, 1)
            tile_out[j] = part.reshape(IMAGES, SLOT, TILE)

        loop(2, give_tile)
        put_rows(sb_0, n // 2, n % 2)
    r_f = exchange(sb_0, rr_f)

    for cp in sum_z:
        cp.wait()
    st_z[z] = stat[:, :, pl.ds(pl.multiple_of(z * TILE, TILE), TILE)]
    st_2[...] = st_z[0] + st_z[1] + st_z[2] + st_z[3]
    sum_x = [
        sems.remote(
            st_2.at[:, :, pl.ds(pl.multiple_of(at(1, off) * TOK, TOK), TOK)],
            st_x.at[x],
            peer(1, off),
        )
        for off in (1, 2, 3)
    ]
    for cp in sum_x:
        cp.start()

    def unpack(way, rr, ag, own, hop, h):
        def summed(s):
            block = rr[h, :, s]
            return dot_tn(onehot[way, h, s], block.reshape(4 * SLOT, HALF))

        s = at(h, 2)
        ag[h, s] = summed(s).astype(bf16)
        copies = []
        for k, off in enumerate((1, 3)):
            cp = sems.remote(ag.at[h, s, pl.ds(64 * k, 64)], hop.at[h, k], peer(h, off))
            cp.start()
            copies.append(cp)
        for off in (1, 3):
            s = at(h, off)
            ag[h, s] = summed(s).astype(bf16)
        own[h] = summed(spot[h])
        return copies

    def pass_on(ag, hop, last, first, h):
        copies = []
        for k, off in enumerate((1, 3)):
            first[k].wait_recv()
            s = at(h, off)
            rows = pl.ds(64 * k, 64)
            ag[h, s, rows] = (ag[h, s, rows].astype(f32) + hop[h, k].astype(f32)).astype(bf16)
            cp = sems.remote(ag.at[h, s], last.at[h, k], peer(h, off))
            cp.start()
            copies.append(cp)
        return copies

    def total_of(own, last, second, h):
        for cp in second:
            cp.wait_recv()
        own[h] += last[h, 0].astype(f32) + last[h, 1].astype(f32)

    arrived(r_b)
    hop_copies_b = [unpack(1, rr_b, ag_xb, own, hop_b, h) for h in (0, 1)]
    last_copies_b = [pass_on(ag_xb, hop_b, last_b, hop_copies_b[h], h) for h in (0, 1)]

    for cp in sum_x:
        cp.wait()
    st_x[x] = st_2[:, :, pl.ds(pl.multiple_of(x * TOK, TOK), TOK)]
    own_part = fin.at[:, :, pl.ds(pl.multiple_of(me * TOK, TOK), TOK)]
    own_part[...] = st_x[0] + st_x[1] + st_x[2] + st_x[3]
    give_x = [sems.remote(own_part, own_part, peer(1, off)) for off in (1, 2, 3)]
    for cp in give_x:
        cp.start()

    for h in (0, 1):
        total_of(own, last_b, last_copies_b[h], h)
    own_scale = modulation_of(1, me // 2, 1)

    def input_grads(c):
        at_rows = pl.ds(pl.multiple_of(c * 32, 32), 32)
        parts = []
        for h in (0, 1):
            parts.append(ag_xb[h, spot[h], at_rows].astype(f32))
        total = jnp.sum(parts[0], axis=1, keepdims=True) + jnp.sum(parts[1], axis=1, keepdims=True)
        center = total * (1.0 / D)
        parts = [part - center for part in parts]
        total = jnp.sum(parts[0] * parts[0], axis=1, keepdims=True) + jnp.sum(
            parts[1] * parts[1], axis=1, keepdims=True
        )
        inv = lax.rsqrt(total * (1.0 / D) + epsilon)
        normed = [part * inv for part in parts]
        grads = []
        for h in (0, 1):
            span = slice(h * HALF, (h + 1) * HALF)
            grads.append(own[h, at_rows] * (1.0 + own_scale[:, span]))
        mean = (
            jnp.sum(grads[0], axis=1, keepdims=True) + jnp.sum(grads[1], axis=1, keepdims=True)
        ) * (1.0 / D)
        slope = (
            jnp.sum(grads[0] * normed[0], axis=1, keepdims=True)
            + jnp.sum(grads[1] * normed[1], axis=1, keepdims=True)
        ) * (1.0 / D)
        for h in (0, 1):
            span = slice(h * HALF, (h + 1) * HALF)
            dyv = ag_dy[h, spot[h], at_rows].astype(f32)
            part = dyv + inv * (grads[h] - mean - normed[h] * slope)
            res[at_rows, span] = part.astype(bf16)

    loop(4, input_grads)
    back_copy = sems.copy(res, out_b)
    back_copy.start()

    for cp in give_x:
        cp.wait()
    own_part = fin.at[:, :, pl.ds(pl.multiple_of(z * TILE, TILE), TILE)]
    give_z = [sems.remote(own_part, own_part, peer(0, off)) for off in (1, 2, 3)]
    for cp in give_z:
        cp.start()

    arrived(r_f)
    hop_copies_f = [unpack(0, rr_f, ag_xf, own, hop_f, h) for h in (0, 1)]
    last_copies_f = [pass_on(ag_xf, hop_f, last_f, hop_copies_f[h], h) for h in (0, 1)]
    for h in (0, 1):
        total_of(own, last_f, last_copies_f[h], h)
    back_copy.wait()
    own_gate = modulation_of(0, me // 2, 2)

    def outputs(c):
        at_rows = pl.ds(pl.multiple_of(c * 32, 32), 32)
        for h in (0, 1):
            span = slice(h * HALF, (h + 1) * HALF)
            part = ag_xf[h, spot[h], at_rows].astype(f32) + own_gate[:, span] * own[h, at_rows]
            res[at_rows, span] = part.astype(bf16)

    loop(4, outputs)
    front_copy = sems.copy(res, out_f)
    front_copy.start()
    for cp in give_z:
        cp.wait()
    fin_copy = sems.copy(fin, fin_out)
    fin_copy.start()
    for cp in r_b[0] + r_f[0]:
        cp.wait_send()
    for pair in hop_copies_b + last_copies_b + hop_copies_f + last_copies_f:
        for cp in pair:
            cp.wait_send()
    front_copy.wait()
    fin_copy.wait()


def layer(routes_f, routes_b, times_f, times_b, table, router, xf, xb, dy, up, down):
    any_spec = pl.BlockSpec(memory_space=pl.ANY)
    vmem = pl.BlockSpec(memory_space=pltpu.VMEM)
    smem = pl.BlockSpec(memory_space=pltpu.SMEM)
    shape = jax.ShapeDtypeStruct
    gather = pltpu.VMEM((2, 4, TOK, HALF), bf16)
    slots = pltpu.VMEM((2, 4, 4, SLOT, HALF), bf16)
    return pl.pallas_call(
        layer_kernel,
        out_shape=(
            shape((TOK, D), bf16),
            shape((TOK, D), bf16),
            shape((2, IMAGES, SLOT, D), bf16),
            shape((2, IMAGES, SLOT, D), bf16),
            shape((2, ROWS, FF), bf16),
            shape((2, ROWS, FF), bf16),
            shape((7, 8, D), f32),
        ),
        in_specs=[vmem, vmem, smem, smem, vmem, vmem] + [any_spec] * 5,
        out_specs=tuple([any_spec] * 7),
        scratch_shapes=[
            pltpu.SemaphoreType.DMA((N_REMOTE,)),
            pltpu.SemaphoreType.DMA((N_REMOTE,)),
            pltpu.SemaphoreType.DMA((N_LOCAL,)),
            pltpu.VMEM((4, 4, 8, TOK), f32),
            pltpu.VMEM((2, 2, 4, 4 * SLOT, TOK), bf16),
            gather,
            gather,
            gather,
            slots,
            slots,
            slots,
            slots,
            slots,
            slots,
            slots,
            pltpu.VMEM((2, 2, 64, HALF), bf16),
            pltpu.VMEM((2, 2, 64, HALF), bf16),
            pltpu.VMEM((2, 2, TOK, HALF), bf16),
            pltpu.VMEM((2, 2, TOK, HALF), bf16),
            pltpu.VMEM((2, TOK, HALF), f32),
            pltpu.VMEM((2, FF, D), bf16),
            pltpu.VMEM((2, FF, D), bf16),
            pltpu.VMEM((2, IMAGES, SLOT, D), bf16),
            pltpu.VMEM((2, IMAGES, SLOT, D), bf16),
            pltpu.VMEM((2, ROWS, FF), f32),
            pltpu.VMEM((2, ROWS, FF), bf16),
            pltpu.VMEM((2, ROWS, FF), bf16),
            pltpu.VMEM((2, IMAGES, SLOT, TILE), f32),
            pltpu.VMEM((3, 2 * IMAGES, D), f32),
            pltpu.VMEM((2, IMAGES, SLOT, 8), f32),
            pltpu.VMEM((2, 2, ROWS, EXPERTS), bf16),
            pltpu.VMEM((7, 8, D), f32),
            pltpu.VMEM((4, 7, 8, TILE), f32),
            pltpu.VMEM((7, 8, TILE), f32),
            pltpu.VMEM((4, 7, 8, TOK), f32),
            pltpu.VMEM((7, 8, D), f32),
            pltpu.VMEM((TOK, D), bf16),
        ],
        compiler_params=pltpu.CompilerParams(
            collective_id=0, has_side_effects=True, vmem_limit_bytes=63 << 20
        ),
        cost_estimate=pl.CostEstimate(
            flops=13_000_000_000, bytes_accessed=30_000_000, transcendentals=2_000_000
        ),
        name="moe_layer",
    )(routes_f, routes_b, times_f, times_b, table, router, xf, xb, dy, up, down)


def gradients_kernel(times, pg, hid, xm, og, sums, up_out, down_out, router_out, table_out, pg_t, hid_t):
    n = pl.program_id(1)

    @pl.when(n == 0)
    def _():
        pg_t[...] = pg[0].T
        hid_t[...] = hid[0].T

    up_out[0, 0] = dot(pg_t[...], xm[0]).astype(bf16)
    down_out[0, 0] = dot(hid_t[...], og[0]).astype(bf16)

    @pl.when((n == 0) & (pl.program_id(0) == 0))
    def _():
        for k in range(EXPERTS // 8):
            router_out[0, 8 * k : 8 * k + 8] = sums[3 + k]
        steps = lax.broadcasted_iota(jnp.int32, (16, 1), 0)
        for c in range(3):
            total = jnp.zeros((16, D), f32)
            for i in range(IMAGES):
                total += jnp.where(steps == times[0, i], sums[c, i : i + 1, :], 0.0)
            table_out[0, c] = total


def gradients(times, pg, hid, xm, og, sums):
    shape = jax.ShapeDtypeStruct
    whole = lambda j, n: (j, 0, 0)
    part = lambda j, n: (j, 0, n)
    return pl.pallas_call(
        gradients_kernel,
        grid=(2, D // TILE),
        out_shape=(
            shape((1, 2, FF, D), bf16),
            shape((1, 2, FF, D), bf16),
            shape((1, EXPERTS, D), f32),
            shape((1, 3, 16, D), f32),
        ),
        in_specs=[
            pl.BlockSpec(memory_space=pltpu.SMEM),
            pl.BlockSpec((1, ROWS, FF), whole),
            pl.BlockSpec((1, ROWS, FF), whole),
            pl.BlockSpec((1, ROWS, TILE), part),
            pl.BlockSpec((1, ROWS, TILE), part),
            pl.BlockSpec((7, 8, D), lambda j, n: (0, 0, 0)),
        ],
        out_specs=(
            pl.BlockSpec((1, 1, FF, TILE), lambda j, n: (0, j, 0, n)),
            pl.BlockSpec((1, 1, FF, TILE), lambda j, n: (0, j, 0, n)),
            pl.BlockSpec((1, EXPERTS, D), lambda j, n: (0, 0, 0)),
            pl.BlockSpec((1, 3, 16, D), lambda j, n: (0, 0, 0, 0)),
        ),
        scratch_shapes=[pltpu.VMEM((FF, ROWS), bf16), pltpu.VMEM((FF, ROWS), bf16)],
        compiler_params=pltpu.CompilerParams(vmem_limit_bytes=40 << 20),
        cost_estimate=pl.CostEstimate(
            flops=4_500_000_000, bytes_accessed=22_000_000, transcendentals=0
        ),
        name="weight_grads",
    )(times, pg, hid, xm, og, sums)


def passed_along(value, steps):
    count = lax.axis_size("section")
    pairs = [(source, (source + steps) % count) for source in range(count)]
    return lax.ppermute(value, "section", pairs)


def per_device(
    forward_input,
    backward_input,
    backward_grad,
    forward_routes,
    backward_routes,
    forward_times,
    backward_times,
    modulation,
    router_weight,
    expert_up,
    expert_down,
):
    block_out, input_part, rows, out_grad, hidden, pre_grad, sums = layer(
        forward_routes[0].T,
        backward_routes[0].T,
        forward_times,
        backward_times,
        modulation.transpose(0, 2, 1, 3),
        router_weight.transpose(0, 2, 1),
        forward_input,
        backward_input,
        backward_grad,
        expert_up.transpose(0, 1, 3, 2),
        expert_down,
    )
    input_grad = passed_along(input_part, -1)
    forward_output = passed_along(block_out, 1)
    rows = rows.reshape(2, ROWS, D)
    out_grad = out_grad.reshape(2, ROWS, D)
    up_grad, down_grad, router_grad, table_grad = gradients(
        backward_times, pre_grad, hidden, rows, out_grad, sums
    )
    return (
        forward_output[None],
        input_grad[None],
        up_grad.transpose(0, 1, 3, 2),
        down_grad,
        router_grad.transpose(0, 2, 1),
        table_grad.transpose(0, 2, 1, 3),
    )


def solution(mesh):
    placed = (
        P("section", "ep", None),
        P("section", "ep", None),
        P("section", "ep", None),
        P("section", "ep", None),
        P("section", "ep", None),
        P("section", None),
        P("section", None),
        P("section", None, None, None),
        P("section", None, None),
        P("section", "ep", None, None),
        P("section", "ep", None, None),
    )
    return jax.shard_map(
        per_device,
        mesh=mesh,
        in_specs=placed,
        out_specs=(
            P("section", "ep", None),
            P("section", "ep", None),
            P("section", "ep", None, None),
            P("section", "ep", None, None),
            P("section", None, None),
            P("section", None, None, None),
        ),
        check_vma=False,
    )
```

time: 479 us -> 204 us (0.43); the launches traced: 469 us -> 204 us
  waiting for transfers between devices: 237 us -> 0.01 us
  Pallas kernels: 0 us -> 191 us
  matrix products: 65.6 us -> 0 us
  local copies, waits for them, and re-layouts: 74 us -> 8.93 us
  other arithmetic: 40.1 us -> 0 us
  starting transfers between devices: 37.1 us -> 2.96 us
  between operations: 15.1 us -> 0.68 us
    pallas_call x0 -> x2, Pallas kernels: none -> 191 us  [the longest x1 180 us: layer(): pl.pallas_call(layer_kernel, out_shape=(shape((TOK, D), bf16), shape((TOK...]
    all_to_all x7 -> x0, waiting for transfers between devices: 163 us -> none  [the longest x2 69.1 us: per_device(): lax.all_to_all(send_rows, 'ep', split_axis=0, concat_axis=0, tiled=True)]
    psum x1 -> x0, waiting for transfers between devices: 74.4 us -> none  [per_device(): lax.psum(router_part.astype(jnp.bfloat16), 'ep').astype(jnp.float32)]
    dot_general x14 -> x0, matrix products: 65.6 us -> none  [the longest x2 19.2 us: experts_local(): jnp.einsum('sjcf,jfd->sjcd', hidden, down_w, preferred_element_type=jnp.f...]
    all_to_all x7 -> x0, starting transfers between devices: 37 us -> none  [the longest x2 11.7 us: per_device(): lax.all_to_all(send_rows, 'ep', split_axis=0, concat_axis=0, tiled=True)]
    gather x16 -> x0, local copies, waits for them, and re-layouts: 22.6 us -> none  [the longest x4 15.5 us: unpack_slots(): return buffer.reshape(-1, width)[slot_ids]]
    scatter x4 -> x0, local copies, waits for them, and re-layouts: 15 us -> none  [pack_slots(): buffer = jnp.zeros((expert_count * capacity, width), values.dtype).at[slo...]
    reduce_sum x8 -> x0, other arithmetic: 12.5 us -> none  [the longest x1 6.21 us: per_device(): combined_b = jnp.sum(top_probs[:, :, None] * gathered_b, axis=1)]
  transfers between devices with their start and end apart: 10 -> 2, of which waited for: 7 -> 0; matrix products, arithmetic and copies ran while one was open for 32% -> 0% of each run, Pallas kernels for 0% -> 5%
where the time goes in v1:
time: 204 us
  Pallas kernels  191 us (94%)
  local copies, waits for them, and re-layouts  8.93 us (4%)
  starting transfers between devices  2.96 us (1%)
    pallas_call x1, Pallas kernels, layer(): pl.pallas_call(layer_kernel, out_shape=(shape((TOK, D), bf16), shape((TOK...  180 us
    pallas_call x1, Pallas kernels, gradients(): pl.pallas_call(gradients_kernel, grid=(2, D // TILE), out_shape=(shape((1...  11 us
    unnamed x14, local copies, waits for them, and re-layouts  8.93 us
  transfers between devices with their start and end apart: 2, of which 0 were waited for; matrix products, arithmetic and copies ran while one was open for 0% of the time, Pallas kernels for 5%

profile of v1, /device:TPU:0, one launch (start us, length us, event | category | flops | bytes accessed | tf_op | source)
XLA Modules:
  0.0 204.1 jit_solution(10854104381861112868)
XLA Ops:
  0.6 0.0 copy-start
  0.6 180.5 %moe_layer.1 = (bf16[128,2048]{1,0:T(8,128)(2,1)}, bf16[128,2048]{1,0:T(8,128)(2,1)}, bf16[2,8,48,2048]{3,2,1,0:T(8,128)(2,1)}, bf16[2,8,48,2048]{3,2,1,0:T(8,12...) custom-call(s32[2,128]{1,0:T(2,128)} %bitcast.23, s32[2,128]{1,0:T(2,128)} %bitcast.24, ...), custom_call_target="tpu_custom_call" | custom-call | flops 12999999488 | bytes 30000000 | tf_op jit(solution)/shard_map/moe_layer/pallas_call | solution.py:681
  181.1 0.0 collective-permute-start
  181.2 2.9 %collective-permute-start.1 = (bf16[128,2048]{1,0:T(8,128)(2,1)}, bf16[128,2048]{1,0:T(8,128)(2,1)S(1)}, u32[]{:S(2)}, u32[]{:S(2)}) collective-permute-start(bf16[128,2048]{1,0:T(8,128)(2,1)} %get-tuple-element.18), channel_id=1, source_target_pairs={{0,112},{16,0},{32,16},{48,32},{64,48},{80,64},{96,80},{112,96},{1... | collective-permute-start | bytes 1572872 | tf_op jit(solution)/shard_map/ppermute | solution.py:805
  184.1 0.0 copy-done
  184.1 0.0 copy-start.1
  184.1 1.9 copy-done.1
  186.0 0.0 copy-start.2
  186.0 1.9 copy-done.2
  187.9 0.0 copy-start.3
  187.9 1.3 copy-done.3
  189.2 0.0 copy-start.4
  189.2 1.3 copy-done.4
  190.4 0.0 copy-start.5
  190.4 1.0 copy-done.5
  191.5 11.0 %weight_grads.1 = (bf16[1,2,704,2048]{3,2,1,0:T(8,128)(2,1)}, bf16[1,2,704,2048]{3,2,1,0:T(8,128)(2,1)}, f32[1,32,2048]{2,1,0:T(8,128)}, f32[1,3,16,2048]{3,2,1,0:T(8,128)}) custom-call(s32[1,8]{1,0:T(1,128)S(1)} %copy-done, bf16[2,384,704]{2,1,0:T(8,128)(2,1)S(1)} %copy-done.4, bf16[2,384,704]{2,1,0:T(8,128)(2,1)S(1)} %copy-done.3, ...), custom_call_target="tpu_custom_call" | custom-call | flops 4499999744 | bytes 22000000 | tf_op jit(solution)/shard_map/weight_grads/pallas_call | solution.py:770
  202.5 0.0 collective-permute-done
  202.5 0.0 collective-permute-done.1
  202.5 0.8 copy.19
  203.3 0.8 copy.20
Async XLA Ops:
  0.6 183.5 %copy-start = (s32[1,8]{1,0:T(1,128)S(1)}, s32[1,8]{1,0:T(1,128)}, u32[]{:S(2)}) copy-start(s32[1,8]{1,0:T(1,128)} %times.1) | copy-start | bytes 100
  181.1 21.3 %collective-permute-start = (bf16[128,2048]{1,0:T(8,128)(2,1)}, bf16[128,2048]{1,0:T(8,128)(2,1)S(1)}, u32[]{:S(2)}, u32[]{:S(2)}) collective-permute-start(bf16[128,2048]{1,0:T(8,128)(2,1)} %get-tuple-element.17), channel_id=1, source_target_pairs={{0,16},{16,32},{32,48},{48,64},{64,80},{80,96},{96,112},{112,0},{1... | collective-permute-start | bytes 1572872 | tf_op jit(solution)/shard_map/ppermute | solution.py:805
  181.2 21.3 %collective-permute-start.1 = (bf16[128,2048]{1,0:T(8,128)(2,1)}, bf16[128,2048]{1,0:T(8,128)(2,1)S(1)}, u32[]{:S(2)}, u32[]{:S(2)}) collective-permute-start(bf16[128,2048]{1,0:T(8,128)(2,1)} %get-tuple-element.18), channel_id=1, source_target_pairs={{0,112},{16,0},{32,16},{48,32},{64,48},{80,64},{96,80},{112,96},{1... | collective-permute-start | bytes 1572872 | tf_op jit(solution)/shard_map/ppermute | solution.py:805
  184.1 1.9 copy-start.1
  186.0 1.9 copy-start.2
  187.9 1.3 copy-start.3
  189.2 1.3 copy-start.4
  190.4 1.0 copy-start.5

commit v2 on v1

--- a/solution.py
+++ b/solution.py
@@ -21,7 +21,7 @@
 f32 = jnp.float32
 bf16 = jnp.bfloat16
 FF_TILES = ((0, 256), (256, 512), (512, 704))
-PROB, PROB2, OTHER, MU, ISTD, PGRAD = (slice(k, k + 1) for k in range(6))
+PROB, PROB2, OTHER, PGRAD, MU_B, ISTD_B = (slice(k, k + 1) for k in range(6))
 GELU_A = 0.7978845608028654
 GELU_B = 0.044715
 
@@ -81,7 +81,7 @@
         return pltpu.make_async_copy(src, dst, self.local.at[k])
 
 
-N_REMOTE = 110
+N_REMOTE = 200
 N_LOCAL = 40
 
 
@@ -262,65 +262,74 @@
 
         loop(4, one)
 
+    def pack(way, ag, sb, h, s):
+        for n in (0, 1):
+            part = dot(onehot[way, h, s], ag[h, s, :, n * TILE : (n + 1) * TILE])
+            sb[h, :, s, :, n * TILE : (n + 1) * TILE] = part.astype(bf16).reshape(4, SLOT, TILE)
+
+    def send_block(sb, rb, h, rel, copies):
+        axis, s = 1 - h, at(h, rel)
+        copies[h, rel] = []
+        for off in (2, 1, 3):
+            cp = sems.remote(
+                sb.at[h, at(axis, off), s], rb.at[h, spot[axis], s], peer(axis, off)
+            )
+            cp.start()
+            copies[h, rel].append(cp)
+
+    def keep_own(sb, rb, h, copies):
+        axis = 1 - h
+        cp = sems.copy(sb.at[h, spot[axis]], rb.at[h, spot[axis]])
+        cp.start()
+        copies[h] = cp
+
+    def pack_send(way, ag, sb, rb, rel, copies):
+        for h in (0, 1):
+            pack(way, ag, sb, h, at(h, rel))
+            send_block(sb, rb, h, rel, copies)
+
+    def all_sent(copies):
+        for h in (0, 1):
+            copies[h].wait()
+            for rel in range(4):
+                for cp in copies[h, rel]:
+                    cp.wait_send()
+
+    def all_arrived(copies):
+        for h in (0, 1):
+            for rel in range(4):
+                for cp in copies[h, rel]:
+                    cp.wait_recv()
+
+    def received(copies):
+        for cp in copies:
+            cp.wait_recv()
+
+    def sent(copies):
+        for cp in copies:
+            cp.wait_send()
+
     build_onehot(1, 0)
     for cp in meta_x:
         cp.wait()
     build_onehot(1, 1)
+    d_xb, d_dy, d_xf = {}, {}, {}
+    f_xb = gather_forward(ag_xb, g_xb)
+    for rel in (0, 1, 3):
+        pack_send(1, ag_xb, sb_0, sl_xb, rel, d_xb)
+    f_dy = gather_forward(ag_dy, g_dy)
+    received(f_xb)
+    pack_send(1, ag_xb, sb_0, sl_xb, 2, d_xb)
+    for rel in (0, 1, 3):
+        pack_send(1, ag_dy, sb_1, sl_dy, rel, d_dy)
+    received(f_dy)
+    pack_send(1, ag_dy, sb_1, sl_dy, 2, d_dy)
+    g_xf = gather_start(ag_xf)
+    for h in (0, 1):
+        keep_own(sb_0, sl_xb, h, d_xb)
+        keep_own(sb_1, sl_dy, h, d_dy)
     build_onehot(0, 0)
     build_onehot(0, 1)
-
-    def pack(way, ag, sb, h):
-        def one(s):
-            for n in (0, 1):
-                part = dot(onehot[way, h, s], ag[h, s, :, n * TILE : (n + 1) * TILE])
-                sb[h, :, s, :, n * TILE : (n + 1) * TILE] = part.astype(bf16).reshape(4, SLOT, TILE)
-
-        loop(4, one)
-
-    def exchange(sb, rb):
-        copies = []
-        for off in (2, 1, 3):
-            for h in (0, 1):
-                axis = 1 - h
-                cp = sems.remote(
-                    sb.at[h, at(axis, off)], rb.at[h, spot[axis]], peer(axis, off)
-                )
-                cp.start()
-                copies.append(cp)
-        local = []
-        for h in (0, 1):
-            axis = 1 - h
-            cp = sems.copy(sb.at[h, spot[axis]], rb.at[h, spot[axis]])
-            cp.start()
-            local.append(cp)
-        return copies, local
-
-    def arrived(copies):
-        for cp in copies[0]:
-            cp.wait_recv()
-        for cp in copies[1]:
-            cp.wait()
-
-    def dispatch_pack(way, ag, first, second, sb, rb):
-        for cp in second:
-            cp.wait_recv()
-        for h in (0, 1):
-            pack(way, ag, sb, h)
-        return exchange(sb, rb)
-
-    f_xb = gather_forward(ag_xb, g_xb)
-    g_xf = gather_start(ag_xf)
-    a_xb = dispatch_pack(1, ag_xb, g_xb, f_xb, sb_0, sl_xb)
-    f_dy = gather_forward(ag_dy, g_dy)
-    a_dy = dispatch_pack(1, ag_dy, g_dy, f_dy, sb_1, sl_dy)
-    f_xf = gather_forward(ag_xf, g_xf)
-    for cp in a_xb[0]:
-        cp.wait_send()
-    for cp in a_xb[1]:
-        cp.wait()
-    a_xf = dispatch_pack(0, ag_xf, g_xf, f_xf, sb_0, sl_xf)
-    for cp in g_xb + f_xb + g_dy + f_dy + g_xf + f_xf:
-        cp.wait_send()
 
     def slots_of(sl, h, zi, xi):
         block = sl[h, xi, zi] if h == 0 else sl[h, zi, xi]
@@ -351,8 +360,9 @@
                     span = slice(h * HALF, (h + 1) * HALF)
                     mixed = part * inv * (1.0 + scale[:, span]) + shift[:, span]
                     xm[j, i, :, span] = mixed.astype(bf16)
-                cols[j, i, :, MU] = center
-                cols[j, i, :, ISTD] = inv
+                if way:
+                    cols[j, i, :, MU_B] = center
+                    cols[j, i, :, ISTD_B] = inv
                 ids = (cap_rows + (me * SLOT + j * CAP)).astype(f32)
                 found = []
                 for par in (0, 1):
@@ -405,39 +415,50 @@
 
         loop(IMAGES, one)
 
-    for cp in a_xb[0]:
-        cp.wait_recv()
+    all_arrived(d_xb)
+    all_sent(d_xb)
+    sent(g_xb + f_xb)
     normalize(sl_xb, 1)
+    f_xf = gather_forward(ag_xf, g_xf)
     up_copy.wait()
     experts_up(True)
     down_copy.wait()
-    arrived(a_dy)
-
-    stat[...] = jnp.zeros_like(stat)
+
+    def out_place(j, i):
+        return 2 * j + i // 4, i % 4
+
+    for n in range(D // TILE):
+        h, inner = n // 2, slice((n % 2) * TILE, (n % 2 + 1) * TILE)
+
+        def out_tile(j):
+            part = dot(hid[j], down[j, :, n * TILE : (n + 1) * TILE]).astype(bf16)
+            part = part.reshape(2, 4, SLOT, TILE)
+            for k in (0, 1):
+                sb_0[h, 2 * j + k, :, :, inner] = part[k]
+
+        loop(2, out_tile)
+
+    all_sent(d_dy)
+    sent(g_dy + f_dy)
+    for rel in (0, 1, 3):
+        pack_send(0, ag_xf, sb_1, sl_xf, rel, d_xf)
+    received(f_xf)
+    pack_send(0, ag_xf, sb_1, sl_xf, 2, d_xf)
+    for h in (0, 1):
+        keep_own(sb_1, sl_xf, h, d_xf)
+    all_arrived(d_dy)
+
     cols[:, :, :, PGRAD] = jnp.zeros((2, IMAGES, SLOT, 1), f32)
 
-    def order_dy(i):
-        for j in (0, 1):
-            for h in (0, 1):
-                og[j, i, :, h * HALF : (h + 1) * HALF] = by_expert(sl_dy, h, i, j).astype(bf16)
-
-    loop(IMAGES, order_dy)
-
-    for n in range(D // TILE):
-        span = slice(n * TILE, (n + 1) * TILE)
-
-        def out_tile(j):
-            part = dot(hid[j], down[j, :, span]).astype(bf16).astype(f32)
-            tile_out[j] = part.reshape(IMAGES, SLOT, TILE)
-
-        loop(2, out_tile)
-
-        def out_image(i):
+    def out_image(i):
+        for h in (0, 1):
+            span = slice(h * HALF, (h + 1) * HALF)
             gate = modulation_of(1, i, 2, span)
-            total = jnp.zeros((1, TILE), f32)
+            total = jnp.zeros((1, HALF), f32)
             for j in (0, 1):
-                out = tile_out[j, i]
-                dyv = og[j, i, :, span].astype(f32)
+                a, b = out_place(j, i)
+                out = sb_0[h, a, b].astype(f32)
+                dyv = by_expert(sl_dy, h, i, j)
                 chance = cols[j, i, :, PROB]
                 mix = (dyv * gate).astype(bf16).astype(f32)
                 cols[j, i, :, PGRAD] += jnp.sum(out * mix, axis=1, keepdims=True)
@@ -445,7 +466,7 @@
                 og[j, i, :, span] = (chance.astype(bf16).astype(f32) * mix).astype(bf16)
             stat[2, pl.ds(i, 1), span] = total
 
-        loop(IMAGES, out_image)
+    loop(IMAGES, out_image)
 
     def hidden_grad(j):
         rows = og[j].reshape(ROWS, D)
@@ -458,11 +479,8 @@
         wrow[j, 1] = (weight - high.astype(f32)).astype(bf16)
 
     loop(2, hidden_grad)
-    for cp in a_dy[0]:
-        cp.wait_send()
-
+    r_b, r_f = {}, {}
     for n in range(D // TILE):
-        h = n // 2
         span = slice(n * TILE, (n + 1) * TILE)
 
         def grad_tile(j):
@@ -470,39 +488,116 @@
             rows = router_ref[0, :, span]
             part += dot(wrow[j, 0], rows) + dot(wrow[j, 1], rows)
             tile_out[j] = part.reshape(IMAGES, SLOT, TILE)
-            block = xm[j].reshape(ROWS, D)[:, span]
-            rg = dot_tn(wrow[j, 0], block) + dot_tn(wrow[j, 1], block)
-            for k in range(EXPERTS // 8):
-                stat[3 + k, :, span] += rg[8 * k : 8 * k + 8]
 
         loop(2, grad_tile)
-        inner = slice((n % 2) * TILE, (n % 2 + 1) * TILE)
-
-        def grad_image(i):
-            zi, xi = i // 2, 2 * (i % 2)
-            shift = jnp.zeros((1, TILE), f32)
-            scale = jnp.zeros((1, TILE), f32)
-            for par in (0, 1):
-                block = sl_xb[h, xi + par, zi, :, inner] if h == 0 else sl_xb[h, zi, xi + par, :, inner]
-                block = block.astype(f32)
-                for j in (0, 1):
-                    cut = slice(par * CAP, (par + 1) * CAP)
-                    grad = tile_out[j, i][cut]
-                    normed = (block[j * CAP : (j + 1) * CAP] - cols[j, i, cut, MU]) * cols[j, i, cut, ISTD]
-                    shift += jnp.sum(grad, axis=0, keepdims=True)
-                    scale += jnp.sum(grad * normed, axis=0, keepdims=True)
-            stat[0, pl.ds(i, 1), span] = shift
-            stat[1, pl.ds(i, 1), span] = scale
-
-        loop(IMAGES, grad_image)
-        put_rows(sb_1, h, n % 2)
-
-    r_b = exchange(sb_1, rr_b)
+        put_rows(sb_0, n // 2, n % 2)
+        if n % 2:
+            for rel in (2, 1, 3, 0):
+                send_block(sb_0, rr_b, n // 2, rel, r_b)
+            keep_own(sb_0, rr_b, n // 2, r_b)
+
     kept = []
     for source, dest in ((xm, xm_out), (og, og_out), (hid, hid_out), (pgr, pg_out)):
         cp = sems.copy(source, dest)
         cp.start()
         kept.append(cp)
+
+    for n in range(D // TILE):
+        span = slice(n * TILE, (n + 1) * TILE)
+        rg = jnp.zeros((EXPERTS, TILE), f32)
+        for j in (0, 1):
+            block = xm[j, :, :, span].reshape(ROWS, TILE)
+            rg += dot_tn(wrow[j, 0], block) + dot_tn(wrow[j, 1], block)
+        for k in range(EXPERTS // 8):
+            stat[3 + k, :, span] = rg[8 * k : 8 * k + 8]
+
+    all_arrived(d_xf)
+    all_sent(d_xf)
+    sent(g_xf + f_xf)
+    for cp in kept:
+        cp.wait()
+    normalize(sl_xf, 0)
+    experts_up(False)
+    for n in range(D // TILE):
+        span = slice(n * TILE, (n + 1) * TILE)
+
+        def give_tile(j):
+            part = dot(hid[j], down[j, :, span]) * cols[j, :, :, PROB].reshape(ROWS, 1)
+            tile_out[j] = part.reshape(IMAGES, SLOT, TILE)
+
+        loop(2, give_tile)
+        put_rows(sb_1, n // 2, n % 2)
+        if n % 2:
+            for rel in (2, 1, 3, 0):
+                send_block(sb_1, rr_f, n // 2, rel, r_f)
+            keep_own(sb_1, rr_f, n // 2, r_f)
+
+    def summed(way, rr, h, s):
+        block = rr[h, :, s]
+        return dot_tn(onehot[way, h, s], block.reshape(4 * SLOT, HALF))
+
+    def return_far(way, rr, ag, hop, arriving):
+        copies = []
+        for h in (0, 1):
+            arriving[h].wait()
+            received(arriving[h, 2])
+            s = at(h, 2)
+            ag[h, s] = summed(way, rr, h, s).astype(bf16)
+            for k, off in enumerate((1, 3)):
+                cp = sems.remote(ag.at[h, s, pl.ds(64 * k, 64)], hop.at[h, k], peer(h, off))
+                cp.start()
+                copies.append(cp)
+        return copies
+
+    def return_near(way, rr, ag, hop, last, arriving, far):
+        copies = []
+        for h in (0, 1):
+            for k, off in enumerate((1, 3)):
+                received(arriving[h, off])
+                s = at(h, off)
+                part = summed(way, rr, h, s)
+                far[2 * h + k].wait_recv()
+                rows = slice(64 * k, 64 * k + 64)
+                rest = slice(64 * (1 - k), 64 * (1 - k) + 64)
+                ag[h, s, rest] = part[rest].astype(bf16)
+                ag[h, s, rows] = (part[rows] + hop[h, k].astype(f32)).astype(bf16)
+                cp = sems.remote(ag.at[h, s], last.at[h, k], peer(h, off))
+                cp.start()
+                copies.append(cp)
+        return copies
+
+    def return_own(way, rr, arriving):
+        for h in (0, 1):
+            received(arriving[h, 0])
+            own[h] = summed(way, rr, h, spot[h])
+
+    def total_of(last, near):
+        for h in (0, 1):
+            received(near[2 * h : 2 * h + 2])
+            own[h] += last[h, 0].astype(f32) + last[h, 1].astype(f32)
+
+    far_b = return_far(1, rr_b, ag_xb, hop_b, r_b)
+
+    def grad_image(i):
+        zi, xi = i // 2, 2 * (i % 2)
+        for h in (0, 1):
+            span = slice(h * HALF, (h + 1) * HALF)
+            shift = jnp.zeros((1, HALF), f32)
+            scale = jnp.zeros((1, HALF), f32)
+            for par in (0, 1):
+                cut = slice(par * CAP, (par + 1) * CAP)
+                center, inv = [
+                    jnp.concatenate([cols[0, i, cut, k], cols[1, i, cut, k]], axis=0)
+                    for k in (MU_B, ISTD_B)
+                ]
+                grad = slots_of(sb_0, h, zi, xi + par)
+                normed = (slots_of(sl_xb, h, zi, xi + par) - center) * inv
+                shift += jnp.sum(grad, axis=0, keepdims=True)
+                scale += jnp.sum(grad * normed, axis=0, keepdims=True)
+            stat[0, pl.ds(i, 1), span] = shift
+            stat[1, pl.ds(i, 1), span] = scale
+
+    loop(IMAGES, grad_image)
     sum_z = [
         sems.remote(
             stat.at[:, :, pl.ds(pl.multiple_of(at(0, off) * TILE, TILE), TILE)],
@@ -513,24 +608,8 @@
     ]
     for cp in sum_z:
         cp.start()
-
-    arrived(a_xf)
-    for cp in kept:
-        cp.wait()
-    normalize(sl_xf, 0)
-    experts_up(False)
-    for cp in a_xf[0]:
-        cp.wait_send()
-    for n in range(D // TILE):
-        span = slice(n * TILE, (n + 1) * TILE)
-
-        def give_tile(j):
-            part = dot(hid[j], down[j, :, span]) * cols[j, :, :, PROB].reshape(ROWS, 1)
-            tile_out[j] = part.reshape(IMAGES, SLOT, TILE)
-
-        loop(2, give_tile)
-        put_rows(sb_0, n // 2, n % 2)
-    r_f = exchange(sb_0, rr_f)
+    near_b = return_near(1, rr_b, ag_xb, hop_b, last_b, r_b, far_b)
+    return_own(1, rr_b, r_b)
 
     for cp in sum_z:
         cp.wait()
@@ -547,45 +626,7 @@
     for cp in sum_x:
         cp.start()
 
-    def unpack(way, rr, ag, own, hop, h):
-        def summed(s):
-            block = rr[h, :, s]
-            return dot_tn(onehot[way, h, s], block.reshape(4 * SLOT, HALF))
-
-        s = at(h, 2)
-        ag[h, s] = summed(s).astype(bf16)
-        copies = []
-        for k, off in enumerate((1, 3)):
-            cp = sems.remote(ag.at[h, s, pl.ds(64 * k, 64)], hop.at[h, k], peer(h, off))
-            cp.start()
-            copies.append(cp)
-        for off in (1, 3):
-            s = at(h, off)
-            ag[h, s] = summed(s).astype(bf16)
-        own[h] = summed(spot[h])
-        return copies
-
-    def pass_on(ag, hop, last, first, h):
-        copies = []
-        for k, off in enumerate((1, 3)):
-            first[k].wait_recv()
-            s = at(h, off)
-            rows = pl.ds(64 * k, 64)
-            ag[h, s, rows] = (ag[h, s, rows].astype(f32) + hop[h, k].astype(f32)).astype(bf16)
-            cp = sems.remote(ag.at[h, s], last.at[h, k], peer(h, off))
-            cp.start()
-            copies.append(cp)
-        return copies
-
-    def total_of(own, last, second, h):
-        for cp in second:
-            cp.wait_recv()
-        own[h] += last[h, 0].astype(f32) + last[h, 1].astype(f32)
-
-    arrived(r_b)
-    hop_copies_b = [unpack(1, rr_b, ag_xb, own, hop_b, h) for h in (0, 1)]
-    last_copies_b = [pass_on(ag_xb, hop_b, last_b, hop_copies_b[h], h) for h in (0, 1)]
-
+    far_f = return_far(0, rr_f, ag_xf, hop_f, r_f)
     for cp in sum_x:
         cp.wait()
     st_x[x] = st_2[:, :, pl.ds(pl.multiple_of(x * TOK, TOK), TOK)]
@@ -595,8 +636,7 @@
     for cp in give_x:
         cp.start()
 
-    for h in (0, 1):
-        total_of(own, last_b, last_copies_b[h], h)
+    total_of(last_b, near_b)
     own_scale = modulation_of(1, me // 2, 1)
 
     def input_grads(c):
@@ -633,18 +673,15 @@
     back_copy = sems.copy(res, out_b)
     back_copy.start()
 
+    near_f = return_near(0, rr_f, ag_xf, hop_f, last_f, r_f, far_f)
     for cp in give_x:
         cp.wait()
     own_part = fin.at[:, :, pl.ds(pl.multiple_of(z * TILE, TILE), TILE)]
     give_z = [sems.remote(own_part, own_part, peer(0, off)) for off in (1, 2, 3)]
     for cp in give_z:
         cp.start()
-
-    arrived(r_f)
-    hop_copies_f = [unpack(0, rr_f, ag_xf, own, hop_f, h) for h in (0, 1)]
-    last_copies_f = [pass_on(ag_xf, hop_f, last_f, hop_copies_f[h], h) for h in (0, 1)]
-    for h in (0, 1):
-        total_of(own, last_f, last_copies_f[h], h)
+    return_own(0, rr_f, r_f)
+    total_of(last_f, near_f)
     back_copy.wait()
     own_gate = modulation_of(0, me // 2, 2)
 
@@ -662,11 +699,11 @@
         cp.wait()
     fin_copy = sems.copy(fin, fin_out)
     fin_copy.start()
-    for cp in r_b[0] + r_f[0]:
-        cp.wait_send()
-    for pair in hop_copies_b + last_copies_b + hop_copies_f + last_copies_f:
-        for cp in pair:
-            cp.wait_send()
+    for copies in (r_b, r_f):
+        for h in (0, 1):
+            for rel in range(4):
+                sent(copies[h, rel])
+    sent(far_b + near_b + far_f + near_f)
     front_copy.wait()
     fin_copy.wait()
 
@@ -791,7 +828,7 @@
             pl.BlockSpec((1, 3, 16, D), lambda j, n: (0, 0, 0, 0)),
         ),
         scratch_shapes=[pltpu.VMEM((FF, ROWS), bf16), pltpu.VMEM((FF, ROWS), bf16)],
-        compiler_params=pltpu.CompilerParams(vmem_limit_bytes=40 << 20),
+        compiler_params=pltpu.CompilerParams(vmem_limit_bytes=60 << 20),
         cost_estimate=pl.CostEstimate(
             flops=4_500_000_000, bytes_accessed=22_000_000, transcendentals=0
         ),

time: 204 us -> 179 us (0.88)
  Pallas kernels: 191 us -> 173 us
  local copies, waits for them, and re-layouts: 8.93 us -> 1.59 us
    pallas_call x1, Pallas kernels: 180 us -> 159 us  [layer(): pl.pallas_call(layer_kernel, out_shape=(shape((TOK, D), bf16), shape((TOK...]
    unnamed x14 -> x2, local copies, waits for them, and re-layouts: 8.93 us -> 1.59 us
    pallas_call x1, Pallas kernels: 11 us -> 14.2 us  [gradients(): pl.pallas_call(gradients_kernel, grid=(2, D // TILE), out_shape=(shape((1...]
  transfers between devices with their start and end apart: 2 -> 2, of which waited for: 0 -> 0; matrix products, arithmetic and copies ran while one was open for 0% -> 0% of each run, Pallas kernels for 5% -> 8%
where the time goes in v2:
time: 179 us
  Pallas kernels  173 us (97%)
  starting transfers between devices  2.96 us (2%)
    pallas_call x1, Pallas kernels, layer(): pl.pallas_call(layer_kernel, out_shape=(shape((TOK, D), bf16), shape((TOK...  159 us
    pallas_call x1, Pallas kernels, gradients(): pl.pallas_call(gradients_kernel, grid=(2, D // TILE), out_shape=(shape((1...  14.2 us
  transfers between devices with their start and end apart: 2, of which 0 were waited for; matrix products, arithmetic and copies ran while one was open for 0% of the time, Pallas kernels for 8%

profile of v2, /device:TPU:0, one launch (start us, length us, event | category | flops | bytes accessed | tf_op | source)
XLA Modules:
  0.0 178.6 jit_solution(14211714432660347006)
XLA Ops:
  0.6 159.1 %moe_layer.1 = (bf16[128,2048]{1,0:T(8,128)(2,1)}, bf16[128,2048]{1,0:T(8,128)(2,1)}, bf16[2,8,48,2048]{3,2,1,0:T(8,128)(2,1)}, bf16[2,8,48,2048]{3,2,1,0:T(8,12...) custom-call(s32[2,128]{1,0:T(2,128)} %bitcast.21, s32[2,128]{1,0:T(2,128)} %bitcast.22, ...), custom_call_target="tpu_custom_call" | custom-call | flops 12999999488 | bytes 30000000 | tf_op jit(solution)/shard_map/moe_layer/pallas_call | solution.py:718
  159.8 0.0 collective-permute-start
  159.8 2.9 %collective-permute-start.1 = (bf16[128,2048]{1,0:T(8,128)(2,1)}, bf16[128,2048]{1,0:T(8,128)(2,1)S(1)}, u32[]{:S(2)}, u32[]{:S(2)}) collective-permute-start(bf16[128,2048]{1,0:T(8,128)(2,1)} %get-tuple-element.18), channel_id=1, source_target_pairs={{0,112},{16,0},{32,16},{48,32},{64,48},{80,64},{96,80},{112,96},{1... | collective-permute-start | bytes 1572872 | tf_op jit(solution)/shard_map/ppermute | solution.py:842
  162.7 14.2 %weight_grads.1 = (bf16[1,2,704,2048]{3,2,1,0:T(8,128)(2,1)}, bf16[1,2,704,2048]{3,2,1,0:T(8,128)(2,1)}, f32[1,32,2048]{2,1,0:T(8,128)}, f32[1,3,16,2048]{3,2,1,0:T(8,128)}) custom-call(s32[1,8]{1,0:T(1,128)} %times.1, bf16[2,384,704]{2,1,0:T(8,128)(2,1)} %get-tuple-element.19.pg, bf16[2,384,704]{2,1,0:T(8,128)(2,1)} %get-tuple-element.20.hid, ...), custom_call_target="tpu_custom_call" | custom-call | flops 4499999744 | bytes 22000000 | tf_op jit(solution)/shard_map/weight_grads/pallas_call | solution.py:807
  176.9 0.0 collective-permute-done
  177.0 0.0 collective-permute-done.1
  177.0 0.8 copy.19
  177.8 0.8 copy.20
Async XLA Ops:
  159.8 17.2 %collective-permute-start = (bf16[128,2048]{1,0:T(8,128)(2,1)}, bf16[128,2048]{1,0:T(8,128)(2,1)S(1)}, u32[]{:S(2)}, u32[]{:S(2)}) collective-permute-start(bf16[128,2048]{1,0:T(8,128)(2,1)} %get-tuple-element.17), channel_id=1, source_target_pairs={{0,16},{16,32},{32,48},{48,64},{64,80},{80,96},{96,112},{112,0},{1... | collective-permute-start | bytes 1572872 | tf_op jit(solution)/shard_map/ppermute | solution.py:842
  159.8 17.2 %collective-permute-start.1 = (bf16[128,2048]{1,0:T(8,128)(2,1)}, bf16[128,2048]{1,0:T(8,128)(2,1)S(1)}, u32[]{:S(2)}, u32[]{:S(2)}) collective-permute-start(bf16[128,2048]{1,0:T(8,128)(2,1)} %get-tuple-element.18), channel_id=1, source_target_pairs={{0,112},{16,0},{32,16},{48,32},{64,48},{80,64},{96,80},{112,96},{1... | collective-permute-start | bytes 1572872 | tf_op jit(solution)/shard_map/ppermute | solution.py:842

commit v3 on v2

--- a/solution.py
+++ b/solution.py
@@ -157,6 +157,11 @@
     def at(axis, off):
         return lax.rem(spot[axis] + off + 4, 4)
 
+    barrier = pltpu.get_barrier_semaphore()
+    for axis in (0, 1):
+        for off in (1, 2, 3):
+            pl.semaphore_signal(barrier, inc=1, device_id=peer(axis, off), device_id_type=MESH)
+
     own_copies = []
     for source, ag in ((xb_hbm, ag_xb), (dy_hbm, ag_dy), (xf_hbm, ag_xf)):
         for h in (0, 1):
@@ -165,8 +170,6 @@
             own_copies.append(cp)
     up_copy = sems.copy(up_hbm.at[0], up)
     down_copy = sems.copy(down_hbm.at[0], down)
-    up_copy.start()
-    down_copy.start()
 
     expert_rows = lax.broadcasted_iota(jnp.int32, (EXPERTS, TOK), 0).astype(f32)
     earlier = (
@@ -185,18 +188,11 @@
         for k, row in enumerate((s0, s1, e0, e1)):
             meta[x, z, 4 * way + k : 4 * way + k + 1, :] = row
 
-    barrier = pltpu.get_barrier_semaphore()
-    for axis in (0, 1):
-        for off in (1, 2, 3):
-            pl.semaphore_signal(barrier, inc=1, device_id=peer(axis, off), device_id_type=MESH)
     pl.semaphore_wait(barrier, 6)
 
     meta_z = [sems.remote(meta.at[x, z], meta.at[x, z], peer(0, off)) for off in (1, 2, 3)]
     for cp in meta_z:
         cp.start()
-
-    for cp in own_copies:
-        cp.wait()
 
     def gather_start(ag):
         copies = []
@@ -219,14 +215,9 @@
                 copies.append(cp)
         return copies
 
+    for cp in own_copies[0:2]:
+        cp.wait()
     g_xb = gather_start(ag_xb)
-    g_dy = gather_start(ag_dy)
-
-    for cp in meta_z:
-        cp.wait()
-    meta_x = [sems.remote(meta.at[x], meta.at[x], peer(1, off)) for off in (1, 2, 3)]
-    for cp in meta_x:
-        cp.start()
 
     time_rows = lax.broadcasted_iota(jnp.int32, (2 * IMAGES, 16), 0)
     time_of = jnp.zeros((2 * IMAGES, 16), jnp.int32)
@@ -239,6 +230,15 @@
 
     def modulation_of(way, i, c, span=slice(0, D)):
         return modr[c, pl.ds(i + IMAGES * way, 1), span]
+
+    for cp in meta_z:
+        cp.wait()
+    meta_x = [sems.remote(meta.at[x], meta.at[x], peer(1, off)) for off in (1, 2, 3)]
+    for cp in meta_x:
+        cp.start()
+    for cp in own_copies[2:4]:
+        cp.wait()
+    g_dy = gather_start(ag_dy)
 
     slot_rows = lax.broadcasted_iota(jnp.int32, (4 * SLOT, TOK), 0)
 
@@ -309,22 +309,29 @@
         for cp in copies:
             cp.wait_send()
 
+    d_xb, d_dy, d_xf = {}, {}, {}
     build_onehot(1, 0)
-    for cp in meta_x:
-        cp.wait()
-    build_onehot(1, 1)
-    d_xb, d_dy, d_xf = {}, {}, {}
     f_xb = gather_forward(ag_xb, g_xb)
-    for rel in (0, 1, 3):
-        pack_send(1, ag_xb, sb_0, sl_xb, rel, d_xb)
+    for h in (0, 1):
+        if h:
+            for cp in meta_x:
+                cp.wait()
+            build_onehot(1, 1)
+        for rel in (0, 1, 3):
+            pack(1, ag_xb, sb_0, h, at(h, rel))
+            send_block(sb_0, sl_xb, h, rel, d_xb)
     f_dy = gather_forward(ag_dy, g_dy)
     received(f_xb)
     pack_send(1, ag_xb, sb_0, sl_xb, 2, d_xb)
     for rel in (0, 1, 3):
         pack_send(1, ag_dy, sb_1, sl_dy, rel, d_dy)
+    for cp in own_copies[4:6]:
+        cp.wait()
+    g_xf = gather_start(ag_xf)
     received(f_dy)
     pack_send(1, ag_dy, sb_1, sl_dy, 2, d_dy)
-    g_xf = gather_start(ag_xf)
+    up_copy.start()
+    down_copy.start()
     for h in (0, 1):
         keep_own(sb_0, sl_xb, h, d_xb)
         keep_own(sb_1, sl_dy, h, d_dy)
@@ -422,31 +429,38 @@
     f_xf = gather_forward(ag_xf, g_xf)
     up_copy.wait()
     experts_up(True)
+    kept = [sems.copy(xm, xm_out), sems.copy(hid, hid_out)]
+    for cp in kept:
+        cp.start()
     down_copy.wait()
 
-    def out_place(j, i):
-        return 2 * j + i // 4, i % 4
-
     for n in range(D // TILE):
-        h, inner = n // 2, slice((n % 2) * TILE, (n % 2 + 1) * TILE)
+        span = slice(n * TILE, (n + 1) * TILE)
 
         def out_tile(j):
-            part = dot(hid[j], down[j, :, n * TILE : (n + 1) * TILE]).astype(bf16)
-            part = part.reshape(2, 4, SLOT, TILE)
-            for k in (0, 1):
-                sb_0[h, 2 * j + k, :, :, inner] = part[k]
+            part = dot(hid[j], down[j, :, span]).astype(bf16)
+            og[j, :, :, span] = part.reshape(IMAGES, SLOT, TILE)
 
         loop(2, out_tile)
 
-    all_sent(d_dy)
+    for h in (0, 1):
+        for rel in (0, 1, 3):
+            pack(0, ag_xf, sb_0, h, at(h, rel))
+    for rel in (0, 1, 3):
+        for h in (0, 1):
+            sent(d_dy[h, rel])
+    for rel in (0, 1, 3):
+        for h in (0, 1):
+            send_block(sb_0, sl_xf, h, rel, d_xf)
+    received(f_xf)
+    pack_send(0, ag_xf, sb_0, sl_xf, 2, d_xf)
+    for h in (0, 1):
+        keep_own(sb_0, sl_xf, h, d_xf)
+    all_arrived(d_dy)
+    for h in (0, 1):
+        d_dy[h].wait()
+        sent(d_dy[h, 2])
     sent(g_dy + f_dy)
-    for rel in (0, 1, 3):
-        pack_send(0, ag_xf, sb_1, sl_xf, rel, d_xf)
-    received(f_xf)
-    pack_send(0, ag_xf, sb_1, sl_xf, 2, d_xf)
-    for h in (0, 1):
-        keep_own(sb_1, sl_xf, h, d_xf)
-    all_arrived(d_dy)
 
     cols[:, :, :, PGRAD] = jnp.zeros((2, IMAGES, SLOT, 1), f32)
 
@@ -456,8 +470,7 @@
             gate = modulation_of(1, i, 2, span)
             total = jnp.zeros((1, HALF), f32)
             for j in (0, 1):
-                a, b = out_place(j, i)
-                out = sb_0[h, a, b].astype(f32)
+                out = og[j, i, :, span].astype(f32)
                 dyv = by_expert(sl_dy, h, i, j)
                 chance = cols[j, i, :, PROB]
                 mix = (dyv * gate).astype(bf16).astype(f32)
@@ -490,17 +503,15 @@
             tile_out[j] = part.reshape(IMAGES, SLOT, TILE)
 
         loop(2, grad_tile)
-        put_rows(sb_0, n // 2, n % 2)
+        put_rows(sb_1, n // 2, n % 2)
         if n % 2:
             for rel in (2, 1, 3, 0):
-                send_block(sb_0, rr_b, n // 2, rel, r_b)
-            keep_own(sb_0, rr_b, n // 2, r_b)
-
-    kept = []
-    for source, dest in ((xm, xm_out), (og, og_out), (hid, hid_out), (pgr, pg_out)):
-        cp = sems.copy(source, dest)
+                send_block(sb_1, rr_b, n // 2, rel, r_b)
+            keep_own(sb_1, rr_b, n // 2, r_b)
+
+    kept_late = [sems.copy(og, og_out), sems.copy(pgr, pg_out)]
+    for cp in kept_late:
         cp.start()
-        kept.append(cp)
 
     for n in range(D // TILE):
         span = slice(n * TILE, (n + 1) * TILE)
@@ -526,11 +537,10 @@
             tile_out[j] = part.reshape(IMAGES, SLOT, TILE)
 
         loop(2, give_tile)
-        put_rows(sb_1, n // 2, n % 2)
+        put_rows(sb_0, n // 2, n % 2)
         if n % 2:
-            for rel in (2, 1, 3, 0):
-                send_block(sb_1, rr_f, n // 2, rel, r_f)
-            keep_own(sb_1, rr_f, n // 2, r_f)
+            send_block(sb_0, rr_f, n // 2, 2, r_f)
+            keep_own(sb_0, rr_f, n // 2, r_f)
 
     def summed(way, rr, h, s):
         block = rr[h, :, s]
@@ -590,7 +600,7 @@
                     jnp.concatenate([cols[0, i, cut, k], cols[1, i, cut, k]], axis=0)
                     for k in (MU_B, ISTD_B)
                 ]
-                grad = slots_of(sb_0, h, zi, xi + par)
+                grad = slots_of(sb_1, h, zi, xi + par)
                 normed = (slots_of(sl_xb, h, zi, xi + par) - center) * inv
                 shift += jnp.sum(grad, axis=0, keepdims=True)
                 scale += jnp.sum(grad * normed, axis=0, keepdims=True)
@@ -608,8 +618,10 @@
     ]
     for cp in sum_z:
         cp.start()
+    for h in (0, 1):
+        for rel in (1, 3):
+            send_block(sb_0, rr_f, h, rel, r_f)
     near_b = return_near(1, rr_b, ag_xb, hop_b, last_b, r_b, far_b)
-    return_own(1, rr_b, r_b)
 
     for cp in sum_z:
         cp.wait()
@@ -627,6 +639,9 @@
         cp.start()
 
     far_f = return_far(0, rr_f, ag_xf, hop_f, r_f)
+    for h in (0, 1):
+        send_block(sb_0, rr_f, h, 0, r_f)
+    return_own(1, rr_b, r_b)
     for cp in sum_x:
         cp.wait()
     st_x[x] = st_2[:, :, pl.ds(pl.multiple_of(x * TOK, TOK), TOK)]
@@ -636,7 +651,14 @@
     for cp in give_x:
         cp.start()
 
+    near_f = return_near(0, rr_f, ag_xf, hop_f, last_f, r_f, far_f)
     total_of(last_b, near_b)
+    for cp in give_x:
+        cp.wait()
+    own_part = fin.at[:, :, pl.ds(pl.multiple_of(z * TILE, TILE), TILE)]
+    give_z = [sems.remote(own_part, own_part, peer(0, off)) for off in (1, 2, 3)]
+    for cp in give_z:
+        cp.start()
     own_scale = modulation_of(1, me // 2, 1)
 
     def input_grads(c):
@@ -673,13 +695,6 @@
     back_copy = sems.copy(res, out_b)
     back_copy.start()
 
-    near_f = return_near(0, rr_f, ag_xf, hop_f, last_f, r_f, far_f)
-    for cp in give_x:
-        cp.wait()
-    own_part = fin.at[:, :, pl.ds(pl.multiple_of(z * TILE, TILE), TILE)]
-    give_z = [sems.remote(own_part, own_part, peer(0, off)) for off in (1, 2, 3)]
-    for cp in give_z:
-        cp.start()
     return_own(0, rr_f, r_f)
     total_of(last_f, near_f)
     back_copy.wait()
@@ -704,6 +719,8 @@
             for rel in range(4):
                 sent(copies[h, rel])
     sent(far_b + near_b + far_f + near_f)
+    for cp in kept_late:
+        cp.wait()
     front_copy.wait()
     fin_copy.wait()
 
@@ -806,7 +823,7 @@
     part = lambda j, n: (j, 0, n)
     return pl.pallas_call(
         gradients_kernel,
-        grid=(2, D // TILE),
+        grid=(2, 2),
         out_shape=(
             shape((1, 2, FF, D), bf16),
             shape((1, 2, FF, D), bf16),
@@ -817,13 +834,13 @@
             pl.BlockSpec(memory_space=pltpu.SMEM),
             pl.BlockSpec((1, ROWS, FF), whole),
             pl.BlockSpec((1, ROWS, FF), whole),
-            pl.BlockSpec((1, ROWS, TILE), part),
-            pl.BlockSpec((1, ROWS, TILE), part),
+            pl.BlockSpec((1, ROWS, HALF), part),
+            pl.BlockSpec((1, ROWS, HALF), part),
             pl.BlockSpec((7, 8, D), lambda j, n: (0, 0, 0)),
         ],
         out_specs=(
-            pl.BlockSpec((1, 1, FF, TILE), lambda j, n: (0, j, 0, n)),
-            pl.BlockSpec((1, 1, FF, TILE), lambda j, n: (0, j, 0, n)),
+            pl.BlockSpec((1, 1, FF, HALF), lambda j, n: (0, j, 0, n)),
+            pl.BlockSpec((1, 1, FF, HALF), lambda j, n: (0, j, 0, n)),
             pl.BlockSpec((1, EXPERTS, D), lambda j, n: (0, 0, 0)),
             pl.BlockSpec((1, 3, 16, D), lambda j, n: (0, 0, 0, 0)),
         ),

time: 179 us -> 171 us (0.955)
  Pallas kernels: 173 us -> 166 us
    pallas_call x1, Pallas kernels: 159 us -> 153 us  [layer(): pl.pallas_call(layer_kernel, out_shape=(shape((TOK, D), bf16), shape((TOK...]
where the time goes in v3:
time: 171 us
  Pallas kernels  166 us (97%)
  starting transfers between devices  2.96 us (2%)
    pallas_call x1, Pallas kernels, layer(): pl.pallas_call(layer_kernel, out_shape=(shape((TOK, D), bf16), shape((TOK...  153 us
    pallas_call x1, Pallas kernels, gradients(): pl.pallas_call(gradients_kernel, grid=(2, 2), out_shape=(shape((1, 2, FF,...  12.9 us
  transfers between devices with their start and end apart: 2, of which 0 were waited for; matrix products, arithmetic and copies ran while one was open for 0% of the time, Pallas kernels for 8%

profile of v3, /device:TPU:0, one launch (start us, length us, event | category | flops | bytes accessed | tf_op | source)
XLA Modules:
  0.0 171.2 jit_solution(9413002410929603696)
XLA Ops:
  0.6 153.1 %moe_layer.1 = (bf16[128,2048]{1,0:T(8,128)(2,1)}, bf16[128,2048]{1,0:T(8,128)(2,1)}, bf16[2,8,48,2048]{3,2,1,0:T(8,128)(2,1)}, bf16[2,8,48,2048]{3,2,1,0:T(8,12...) custom-call(s32[2,128]{1,0:T(2,128)} %bitcast.21, s32[2,128]{1,0:T(2,128)} %bitcast.22, ...), custom_call_target="tpu_custom_call" | custom-call | flops 12999999488 | bytes 30000000 | tf_op jit(solution)/shard_map/moe_layer/pallas_call | solution.py:735
  153.8 0.0 collective-permute-start
  153.8 2.9 %collective-permute-start.1 = (bf16[128,2048]{1,0:T(8,128)(2,1)}, bf16[128,2048]{1,0:T(8,128)(2,1)S(1)}, u32[]{:S(2)}, u32[]{:S(2)}) collective-permute-start(bf16[128,2048]{1,0:T(8,128)(2,1)} %get-tuple-element.18), channel_id=1, source_target_pairs={{0,112},{16,0},{32,16},{48,32},{64,48},{80,64},{96,80},{112,96},{1... | collective-permute-start | bytes 1572872 | tf_op jit(solution)/shard_map/ppermute | solution.py:859
  156.7 12.9 %weight_grads.1 = (bf16[1,2,704,2048]{3,2,1,0:T(8,128)(2,1)}, bf16[1,2,704,2048]{3,2,1,0:T(8,128)(2,1)}, f32[1,32,2048]{2,1,0:T(8,128)}, f32[1,3,16,2048]{3,2,1,0:T(8,128)}) custom-call(s32[1,8]{1,0:T(1,128)} %times.1, bf16[2,384,704]{2,1,0:T(8,128)(2,1)} %get-tuple-element.19.pg, bf16[2,384,704]{2,1,0:T(8,128)(2,1)} %get-tuple-element.20.hid, ...), custom_call_target="tpu_custom_call" | custom-call | flops 4499999744 | bytes 22000000 | tf_op jit(solution)/shard_map/weight_grads/pallas_call | solution.py:824
  169.6 0.0 collective-permute-done
  169.6 0.0 collective-permute-done.1
  169.6 0.8 copy.19
  170.4 0.8 copy.20
Async XLA Ops:
  153.8 15.8 %collective-permute-start = (bf16[128,2048]{1,0:T(8,128)(2,1)}, bf16[128,2048]{1,0:T(8,128)(2,1)S(1)}, u32[]{:S(2)}, u32[]{:S(2)}) collective-permute-start(bf16[128,2048]{1,0:T(8,128)(2,1)} %get-tuple-element.17), channel_id=1, source_target_pairs={{0,16},{16,32},{32,48},{48,64},{64,80},{80,96},{96,112},{112,0},{1... | collective-permute-start | bytes 1572872 | tf_op jit(solution)/shard_map/ppermute | solution.py:859
  153.8 15.8 %collective-permute-start.1 = (bf16[128,2048]{1,0:T(8,128)(2,1)}, bf16[128,2048]{1,0:T(8,128)(2,1)S(1)}, u32[]{:S(2)}, u32[]{:S(2)}) collective-permute-start(bf16[128,2048]{1,0:T(8,128)(2,1)} %get-tuple-element.18), channel_id=1, source_target_pairs={{0,112},{16,0},{32,16},{48,32},{64,48},{80,64},{96,80},{112,96},{1... | collective-permute-start | bytes 1572872 | tf_op jit(solution)/shard_map/ppermute | solution.py:859

commit v4 on v3

--- a/solution.py
+++ b/solution.py
@@ -194,12 +194,12 @@
     for cp in meta_z:
         cp.start()
 
-    def gather_start(ag):
+    def gather_start(ag, source):
         copies = []
         for off in (1, 3):
             for h in (0, 1):
-                block = ag.at[h, spot[h]]
-                cp = sems.remote(block, block, peer(h, off))
+                rows = source.at[0, :, pl.ds(h * HALF, HALF)]
+                cp = sems.remote(rows, ag.at[h, spot[h]], peer(h, off))
                 cp.start()
                 copies.append(cp)
         return copies
@@ -215,9 +215,7 @@
                 copies.append(cp)
         return copies
 
-    for cp in own_copies[0:2]:
-        cp.wait()
-    g_xb = gather_start(ag_xb)
+    g_xb = gather_start(ag_xb, xb_hbm)
 
     time_rows = lax.broadcasted_iota(jnp.int32, (2 * IMAGES, 16), 0)
     time_of = jnp.zeros((2 * IMAGES, 16), jnp.int32)
@@ -236,9 +234,9 @@
     meta_x = [sems.remote(meta.at[x], meta.at[x], peer(1, off)) for off in (1, 2, 3)]
     for cp in meta_x:
         cp.start()
-    for cp in own_copies[2:4]:
+    g_dy = gather_start(ag_dy, dy_hbm)
+    for cp in own_copies:
         cp.wait()
-    g_dy = gather_start(ag_dy)
 
     slot_rows = lax.broadcasted_iota(jnp.int32, (4 * SLOT, TOK), 0)
 
@@ -325,9 +323,7 @@
     pack_send(1, ag_xb, sb_0, sl_xb, 2, d_xb)
     for rel in (0, 1, 3):
         pack_send(1, ag_dy, sb_1, sl_dy, rel, d_dy)
-    for cp in own_copies[4:6]:
-        cp.wait()
-    g_xf = gather_start(ag_xf)
+    g_xf = gather_start(ag_xf, xf_hbm)
     received(f_dy)
     pack_send(1, ag_dy, sb_1, sl_dy, 2, d_dy)
     up_copy.start()
@@ -522,72 +518,6 @@
         for k in range(EXPERTS // 8):
             stat[3 + k, :, span] = rg[8 * k : 8 * k + 8]
 
-    all_arrived(d_xf)
-    all_sent(d_xf)
-    sent(g_xf + f_xf)
-    for cp in kept:
-        cp.wait()
-    normalize(sl_xf, 0)
-    experts_up(False)
-    for n in range(D // TILE):
-        span = slice(n * TILE, (n + 1) * TILE)
-
-        def give_tile(j):
-            part = dot(hid[j], down[j, :, span]) * cols[j, :, :, PROB].reshape(ROWS, 1)
-            tile_out[j] = part.reshape(IMAGES, SLOT, TILE)
-
-        loop(2, give_tile)
-        put_rows(sb_0, n // 2, n % 2)
-        if n % 2:
-            send_block(sb_0, rr_f, n // 2, 2, r_f)
-            keep_own(sb_0, rr_f, n // 2, r_f)
-
-    def summed(way, rr, h, s):
-        block = rr[h, :, s]
-        return dot_tn(onehot[way, h, s], block.reshape(4 * SLOT, HALF))
-
-    def return_far(way, rr, ag, hop, arriving):
-        copies = []
-        for h in (0, 1):
-            arriving[h].wait()
-            received(arriving[h, 2])
-            s = at(h, 2)
-            ag[h, s] = summed(way, rr, h, s).astype(bf16)
-            for k, off in enumerate((1, 3)):
-                cp = sems.remote(ag.at[h, s, pl.ds(64 * k, 64)], hop.at[h, k], peer(h, off))
-                cp.start()
-                copies.append(cp)
-        return copies
-
-    def return_near(way, rr, ag, hop, last, arriving, far):
-        copies = []
-        for h in (0, 1):
-            for k, off in enumerate((1, 3)):
-                received(arriving[h, off])
-                s = at(h, off)
-                part = summed(way, rr, h, s)
-                far[2 * h + k].wait_recv()
-                rows = slice(64 * k, 64 * k + 64)
-                rest = slice(64 * (1 - k), 64 * (1 - k) + 64)
-                ag[h, s, rest] = part[rest].astype(bf16)
-                ag[h, s, rows] = (part[rows] + hop[h, k].astype(f32)).astype(bf16)
-                cp = sems.remote(ag.at[h, s], last.at[h, k], peer(h, off))
-                cp.start()
-                copies.append(cp)
-        return copies
-
-    def return_own(way, rr, arriving):
-        for h in (0, 1):
-            received(arriving[h, 0])
-            own[h] = summed(way, rr, h, spot[h])
-
-    def total_of(last, near):
-        for h in (0, 1):
-            received(near[2 * h : 2 * h + 2])
-            own[h] += last[h, 0].astype(f32) + last[h, 1].astype(f32)
-
-    far_b = return_far(1, rr_b, ag_xb, hop_b, r_b)
-
     def grad_image(i):
         zi, xi = i // 2, 2 * (i % 2)
         for h in (0, 1):
@@ -618,10 +548,76 @@
     ]
     for cp in sum_z:
         cp.start()
-    for h in (0, 1):
-        for rel in (1, 3):
-            send_block(sb_0, rr_f, h, rel, r_f)
-    near_b = return_near(1, rr_b, ag_xb, hop_b, last_b, r_b, far_b)
+    all_arrived(d_xf)
+    all_sent(d_xf)
+    sent(g_xf + f_xf)
+    for cp in kept:
+        cp.wait()
+    normalize(sl_xf, 0)
+    experts_up(False)
+    for n in range(D // TILE):
+        span = slice(n * TILE, (n + 1) * TILE)
+
+        def give_tile(j):
+            part = dot(hid[j], down[j, :, span]) * cols[j, :, :, PROB].reshape(ROWS, 1)
+            tile_out[j] = part.reshape(IMAGES, SLOT, TILE)
+
+        loop(2, give_tile)
+        put_rows(sb_0, n // 2, n % 2)
+        if n % 2:
+            send_block(sb_0, rr_f, n // 2, 2, r_f)
+            keep_own(sb_0, rr_f, n // 2, r_f)
+
+    def summed(way, rr, h, s):
+        block = rr[h, :, s]
+        return dot_tn(onehot[way, h, s], block.reshape(4 * SLOT, HALF))
+
+    def return_far(way, rr, ag, hop, arriving):
+        copies = []
+        for h in (0, 1):
+            arriving[h].wait()
+            received(arriving[h, 2])
+            s = at(h, 2)
+            ag[h, s] = summed(way, rr, h, s).astype(bf16)
+            for k, off in enumerate((1, 3)):
+                cp = sems.remote(ag.at[h, s, pl.ds(64 * k, 64)], hop.at[h, k], peer(h, off))
+                cp.start()
+                copies.append(cp)
+        return copies
+
+    def return_near(way, rr, ag, hop, last, arriving, far):
+        copies = []
+        for h in (0, 1):
+            for k, off in enumerate((1, 3)):
+                received(arriving[h, off])
+                s = at(h, off)
+                ag[h, s] = summed(way, rr, h, s).astype(bf16)
+                rest = pl.ds(64 * (1 - k), 64)
+                cp = sems.remote(ag.at[h, s, rest], last.at[h, k, rest], peer(h, off))
+                cp.start()
+                copies.append(cp)
+        for h in (0, 1):
+            for k, off in enumerate((1, 3)):
+                s = at(h, off)
+                far[2 * h + k].wait_recv()
+                rows = pl.ds(64 * k, 64)
+                ag[h, s, rows] = (ag[h, s, rows].astype(f32) + hop[h, k].astype(f32)).astype(bf16)
+                cp = sems.remote(ag.at[h, s, rows], last.at[h, k, rows], peer(h, off))
+                cp.start()
+                copies.append(cp)
+        return copies
+
+    def return_own(way, rr, arriving):
+        for h in (0, 1):
+            received(arriving[h, 0])
+            own[h] = summed(way, rr, h, spot[h])
+
+    def total_of(last, near):
+        received(near)
+        for h in (0, 1):
+            own[h] += last[h, 0].astype(f32) + last[h, 1].astype(f32)
+
+    far_b = return_far(1, rr_b, ag_xb, hop_b, r_b)
 
     for cp in sum_z:
         cp.wait()
@@ -638,10 +634,11 @@
     for cp in sum_x:
         cp.start()
 
-    far_f = return_far(0, rr_f, ag_xf, hop_f, r_f)
     for h in (0, 1):
-        send_block(sb_0, rr_f, h, 0, r_f)
-    return_own(1, rr_b, r_b)
+        for rel in (1, 3):
+            send_block(sb_0, rr_f, h, rel, r_f)
+    near_b = return_near(1, rr_b, ag_xb, hop_b, last_b, r_b, far_b)
+
     for cp in sum_x:
         cp.wait()
     st_x[x] = st_2[:, :, pl.ds(pl.multiple_of(x * TOK, TOK), TOK)]
@@ -651,14 +648,18 @@
     for cp in give_x:
         cp.start()
 
-    near_f = return_near(0, rr_f, ag_xf, hop_f, last_f, r_f, far_f)
-    total_of(last_b, near_b)
+    far_f = return_far(0, rr_f, ag_xf, hop_f, r_f)
+    for h in (0, 1):
+        send_block(sb_0, rr_f, h, 0, r_f)
+    return_own(1, rr_b, r_b)
     for cp in give_x:
         cp.wait()
     own_part = fin.at[:, :, pl.ds(pl.multiple_of(z * TILE, TILE), TILE)]
     give_z = [sems.remote(own_part, own_part, peer(0, off)) for off in (1, 2, 3)]
     for cp in give_z:
         cp.start()
+    near_f = return_near(0, rr_f, ag_xf, hop_f, last_f, r_f, far_f)
+    total_of(last_b, near_b)
     own_scale = modulation_of(1, me // 2, 1)
 
     def input_grads(c):

time: 171 us -> 172 us (level)
  transfers between devices with their start and end apart: 2 -> 2, of which waited for: 0 -> 0; matrix products, arithmetic and copies ran while one was open for 0% -> 0% of each run, Pallas kernels for 8% -> 7%
where the time goes in v4:
time: 172 us
  Pallas kernels  166 us (97%)
  starting transfers between devices  2.96 us (2%)
    pallas_call x1, Pallas kernels, layer(): pl.pallas_call(layer_kernel, out_shape=(shape((TOK, D), bf16), shape((TOK...  154 us
    pallas_call x1, Pallas kernels, gradients(): pl.pallas_call(gradients_kernel, grid=(2, 2), out_shape=(shape((1, 2, FF,...  12.9 us
  transfers between devices with their start and end apart: 2, of which 0 were waited for; matrix products, arithmetic and copies ran while one was open for 0% of the time, Pallas kernels for 7%

profile of v4, /device:TPU:0, one launch (start us, length us, event | category | flops | bytes accessed | tf_op | source)
XLA Modules:
  0.0 171.7 jit_solution(3151058053614333873)
XLA Ops:
  0.6 153.6 %moe_layer.1 = (bf16[128,2048]{1,0:T(8,128)(2,1)}, bf16[128,2048]{1,0:T(8,128)(2,1)}, bf16[2,8,48,2048]{3,2,1,0:T(8,128)(2,1)}, bf16[2,8,48,2048]{3,2,1,0:T(8,12...) custom-call(s32[2,128]{1,0:T(2,128)} %bitcast.21, s32[2,128]{1,0:T(2,128)} %bitcast.22, ...), custom_call_target="tpu_custom_call" | custom-call | flops 12999999488 | bytes 30000000 | tf_op jit(solution)/shard_map/moe_layer/pallas_call | solution.py:736
  154.2 0.0 collective-permute-start
  154.3 2.9 %collective-permute-start.1 = (bf16[128,2048]{1,0:T(8,128)(2,1)}, bf16[128,2048]{1,0:T(8,128)(2,1)S(1)}, u32[]{:S(2)}, u32[]{:S(2)}) collective-permute-start(bf16[128,2048]{1,0:T(8,128)(2,1)} %get-tuple-element.18), channel_id=1, source_target_pairs={{0,112},{16,0},{32,16},{48,32},{64,48},{80,64},{96,80},{112,96},{1... | collective-permute-start | bytes 1572872 | tf_op jit(solution)/shard_map/ppermute | solution.py:860
  157.2 12.9 %weight_grads.1 = (bf16[1,2,704,2048]{3,2,1,0:T(8,128)(2,1)}, bf16[1,2,704,2048]{3,2,1,0:T(8,128)(2,1)}, f32[1,32,2048]{2,1,0:T(8,128)}, f32[1,3,16,2048]{3,2,1,0:T(8,128)}) custom-call(s32[1,8]{1,0:T(1,128)} %times.1, bf16[2,384,704]{2,1,0:T(8,128)(2,1)} %get-tuple-element.19.pg, bf16[2,384,704]{2,1,0:T(8,128)(2,1)} %get-tuple-element.20.hid, ...), custom_call_target="tpu_custom_call" | custom-call | flops 4499999744 | bytes 22000000 | tf_op jit(solution)/shard_map/weight_grads/pallas_call | solution.py:825
  170.1 0.0 collective-permute-done
  170.1 0.0 collective-permute-done.1
  170.1 0.8 copy.19
  170.9 0.8 copy.20
Async XLA Ops:
  154.2 15.8 %collective-permute-start = (bf16[128,2048]{1,0:T(8,128)(2,1)}, bf16[128,2048]{1,0:T(8,128)(2,1)S(1)}, u32[]{:S(2)}, u32[]{:S(2)}) collective-permute-start(bf16[128,2048]{1,0:T(8,128)(2,1)} %get-tuple-element.17), channel_id=1, source_target_pairs={{0,16},{16,32},{32,48},{48,64},{64,80},{80,96},{96,112},{112,0},{1... | collective-permute-start | bytes 1572872 | tf_op jit(solution)/shard_map/ppermute | solution.py:860
  154.3 15.8 %collective-permute-start.1 = (bf16[128,2048]{1,0:T(8,128)(2,1)}, bf16[128,2048]{1,0:T(8,128)(2,1)S(1)}, u32[]{:S(2)}, u32[]{:S(2)}) collective-permute-start(bf16[128,2048]{1,0:T(8,128)(2,1)} %get-tuple-element.18), channel_id=1, source_target_pairs={{0,112},{16,0},{32,16},{48,32},{64,48},{80,64},{96,80},{112,96},{1... | collective-permute-start | bytes 1572872 | tf_op jit(solution)/shard_map/ppermute | solution.py:860
